TPU v7x, 256 devices: a whole 4x4x8 slice. The times are simulated.
256 devices in a mesh: occ: 8 (over x_hi, y), virt: 32 (over z, x_lo, core).
Axes of the slice: x: 4 (x_hi: 2, x_lo: 2; x = x_hi * 2 + x_lo), y: 4, z: 8, core: 2. Of those that a mesh axis runs over, the one named last changes fastest.
Arguments:
- amplitudes: float32 [24, 24, 384, 384], P('occ', None, 'virt'), may hold values from -6 to 6
- cycle_integrals: bfloat16 [384, 24, 24, 384], P('virt', None, 'occ'), may hold values from -0.0625 to 0.0625
- occ_energy: float32 [24], replicated, may hold values from -2 to -0.5
- virt_energy: float32 [384], replicated, may hold values from 0.2 to 1.5
- occ_irrep: int32 [24], replicated, may hold values from 0 to 3
- virt_irrep: int32 [384], replicated, may hold values from 0 to 3, as said below
Outputs:
- new_amplitudes: float32 [24, 24, 384, 384], P('occ', None, 'virt')
Inputs may be any that keep to these rules, and one draw needn't show every extreme that they name: `occ_irrep`: C2v irrep labels; the product of irreps is their exclusive or. `virt_irrep`: C2v irrep labels; the product of irreps is their exclusive or; each of the four irreps labels exactly 96 virtual orbitals.
All inputs are finite; a program needn't handle non-finite values.
Results may differ from a plain program's by a relative error of at most 0.0012.
Values may be sent and summed in bfloat16 or wider, within the bound.
A program may use at most 192 MiB of HBM per device.

v0:
```python
import jax
import jax.numpy as jnp
from jax import lax
from jax.sharding import PartitionSpec as P


def irrep_mask(occ_rows, occ_labels, virt_rows, virt_labels):
    combined = jnp.bitwise_xor(
        jnp.bitwise_xor(occ_rows[:, None, None, None], occ_labels[None, :, None, None]),
        jnp.bitwise_xor(virt_rows[None, None, :, None], virt_labels[None, None, None, :]),
    )
    return (combined == 0).astype(jnp.float32)


def local(amplitudes, cycle_integrals, occ_energy, virt_energy, occ_irrep, virt_irrep):
    occ_dev = amplitudes.shape[0]
    virt_dev = amplitudes.shape[2]
    occ_first = lax.axis_index("occ") * occ_dev
    virt_first = lax.axis_index("virt") * virt_dev
    own_occ = lax.dynamic_slice_in_dim(occ_irrep, occ_first, occ_dev)
    own_virt = lax.dynamic_slice_in_dim(virt_irrep, virt_first, virt_dev)
    allowed = irrep_mask(own_occ, occ_irrep, own_virt, virt_irrep)
    amps_low = (amplitudes * allowed).astype(jnp.bfloat16)
    columns = lax.all_gather(cycle_integrals, "occ", axis=2, tiled=True)
    partial_cycle = jnp.einsum(
        "ikac,bjkc->ibja",
        lax.all_gather(amps_low, "virt", axis=2, tiled=True),
        columns,
        preferred_element_type=jnp.float32,
    )
    regrouped = lax.all_to_all(
        partial_cycle.astype(jnp.bfloat16), "virt", split_axis=3, concat_axis=1, tiled=True
    ).astype(partial_cycle.dtype)
    direct = jnp.transpose(regrouped, (0, 2, 3, 1))
    mirrored = lax.all_to_all(
        direct.astype(jnp.bfloat16), "occ", split_axis=1, concat_axis=0, tiled=True
    ).astype(direct.dtype)
    mirror = jnp.swapaxes(mirrored, 0, 1)
    own_occ_energy = lax.dynamic_slice_in_dim(occ_energy, occ_first, occ_dev)
    own_virt_energy = lax.dynamic_slice_in_dim(virt_energy, virt_first, virt_dev)
    denom = (
        own_occ_energy[:, None, None, None]
        + occ_energy[None, :, None, None]
        - own_virt_energy[None, None, :, None]
        - virt_energy[None, None, None, :]
    )
    return allowed * (amplitudes + (direct - mirror) / denom)


def solution(mesh):
    return jax.shard_map(
        local,
        mesh=mesh,
        in_specs=(P("occ", None, "virt", None), P("virt", None, "occ", None), P(), P(), P(), P()),
        out_specs=P("occ", None, "virt", None),
        check_vma=False,
    )
```

profile of v0, /device:TPU:1, one launch (start us, length us, event | category | flops | bytes accessed | tf_op | source)
XLA Modules:
  0.0 335.1 jit_solution(15600324510255701835)
XLA Ops:
  6.5 0.0 all-gather.5.cloned.1.call-start
  6.5 0.7 all-gather.5.cloned.1.call-update
  7.3 0.0 all-gather.3.cloned.1.call-start
  7.3 0.8 dynamic_slice.13
  8.1 0.7 dynamic_slice.12
  8.8 0.7 broadcast_xor_fusion.1
  9.5 0.8 broadcast_xor_fusion
  10.3 1.6 select_convert_fusion
  11.9 0.9 copy.25
  12.8 0.0 all-gather.3.cloned.1.call-update
  12.8 86.2 %all-gather.5.cloned.1.call-done = bf16[12,24,24,384]{3,1,2,0:T(8,128)(2,1)} async-done(((bf16[12,24,3,384]{3,1,2,0:T(8,128)(2,1)}), bf16[12,24,24,384]{3,1,2,0:T(8,128)(2,1)}) %all-gather.5.cloned.1.call-update) | async-done | bytes 5308432 | tf_op jit(solution)/shard_map/all_gather | solution.py:24
  99.0 122.8 %all-gather.3.cloned.1.call-done = bf16[3,24,384,384]{3,1,0,2:T(8,128)(2,1)} async-done(((bf16[3,24,12,384]{3,1,0,2:T(8,128)(2,1)}), bf16[3,24,384,384]{3,1,0,2:T(8,128)(2,1)}) %all-gather.3.cloned.1.call-update) | async-done | bytes 21233680 | tf_op jit(solution)/shard_map/all_gather | solution.py:27
  221.8 13.7 %fusion.16 = bf16[3,12,24,384]{3,2,1,0:T(8,128)(2,1)S(1)} fusion(bf16[12,24,24,384]{3,1,2,0:T(8,128)(2,1)} %all-gather.5.cloned.1.call-done, bf16[3,24,384,384,1]{3,1,0,2,4:T(8,128)(2,1)} %bitcast.51), kind=kOutput, calls=%fused_computation.12 | convolution fusion | flops 6115627008 | bytes 27205632 | tf_op jit(solution)/shard_map/ikac,bjkc->ibja/dot_general | solution.py:25
  235.5 4.5 %copy.27 = bf16[3,12,24,384]{2,1,0,3:T(8,128)(2,1)} copy(bf16[3,12,24,384]{3,2,1,0:T(8,128)(2,1)S(1)} %fusion.16) | data formatting | bytes 1327104 | tf_op jit(solution)/shard_map/convert_element_type | solution.py:32
  240.0 6.8 %reshape.117 = bf16[32,2,5184]{2,1,0:T(2,128)(2,1)S(1)} reshape(bf16[384,3,12,24]{3,2,1,0:T(8,128)(2,1)} %bitcast.46) | data formatting | bytes 1327104
  246.8 27.1 %all_to_all.8 = bf16[32,2,5184]{2,1,0:T(2,128)(2,1)S(1)} all-to-all(bf16[32,2,5184]{2,1,0:T(2,128)(2,1)S(1)} %reshape.117), channel_id=1, replica_groups=mesh['occ'=8,'virt'=32] {'virt'}, dimensions={0} | all-to-all | bytes 1327104 | tf_op jit(solution)/shard_map/all_to_all | solution.py:31
  273.9 6.1 %reshape.118 = bf16[384,3,12,24]{3,2,1,0:T(8,128)(2,1)} reshape(bf16[32,2,5184]{2,1,0:T(2,128)(2,1)S(1)} %all_to_all.8) | data formatting | bytes 1327104
  279.9 11.2 %copy.29 = bf16[3,32,12,24,12]{2,1,3,4,0:T(8,128)(2,1)} copy(bf16[3,32,12,24,12]{3,2,0,4,1:T(8,128)(2,1)} %bitcast.47) | data formatting | bytes 1327104 | tf_op jit(solution)/shard_map/convert_element_type | solution.py:33
  291.1 12.9 %convert_element_type.36 = bf16[3,384,24,12]{1,2,3,0:T(8,128)(2,1)S(1)} reshape(bf16[3,32,12,24,12]{2,1,3,4,0:T(8,128)(2,1)} %copy.29) | data formatting | bytes 1327104 | tf_op jit(solution)/shard_map/convert_element_type | solution.py:33
  304.1 0.0 copy-start.1
  304.1 0.0 copy-start
  304.1 1.0 copy.30
  305.1 6.1 %all-to-all-start.1 = ((bf16[3,24,12,384]{3,2,0,1:T(8,128)(2,1)}), bf16[3,24,12,384]{3,2,0,1:T(8,128)(2,1)S(1)}, u32[]{:S(2)}, u32[]{:S(2)}) async-start(bf16[3,24,12,384]{3,2,0,1:T(8,128)(2,1)} %copy.30), calls=%async_computation.1 | async-start | bytes 1769472 | tf_op jit(solution)/shard_map/all_to_all | solution.py:35
  311.3 0.0 copy-done.1
  311.3 0.1 dynamic_slice.14
  311.3 0.0 copy-done
  311.3 0.1 dynamic_slice.15
  311.4 0.1 broadcast_add_fusion
  311.5 0.1 broadcast_subtract_fusion
  311.6 11.4 %all-to-all-done.1 = bf16[3,24,12,384]{3,2,0,1:T(8,128)(2,1)S(1)} async-done(((bf16[3,24,12,384]{3,2,0,1:T(8,128)(2,1)}), bf16[3,24,12,384]{3,2,0,1:T(8,128)(2,1)S(1)}, u32[]{:S(2)}, u32[]{:S(2)}) %all-to-all-start.1) | async-done | bytes 663584 | tf_op jit(solution)/shard_map/all_to_all | solution.py:35
  323.0 0.5 copy.47
  323.5 1.5 reshape.112
  325.0 3.2 fusion.15
Async XLA Ops:
  6.5 92.5 %all-gather.5.cloned.1.call-start = ((), (), s32[]{:S(2)}) async-start(), calls=%async_computation.3 | async-start | bytes 5971968 | tf_op jit(solution)/shard_map/all_gather | solution.py:24
  7.3 214.6 %all-gather.3.cloned.1.call-start = ((), (), s32[]{:S(2)}) async-start(), calls=%async_computation.2 | async-start | bytes 21897216 | tf_op jit(solution)/shard_map/all_gather | solution.py:27
  304.1 7.2 %copy-start.1 = (f32[24]{0:T(128)S(1)}, f32[24]{0:T(128)}, u32[]{:S(2)}) copy-start(f32[24]{0:T(128)} %param.8) | copy-start | bytes 292
  304.1 7.3 %copy-start = (f32[384]{0:T(512)S(1)}, f32[384]{0:T(512)}, u32[]{:S(2)}) copy-start(f32[384]{0:T(512)} %param.9) | copy-start | bytes 4612
  305.1 17.9 %all-to-all-start.1 = ((bf16[3,24,12,384]{3,2,0,1:T(8,128)(2,1)}), bf16[3,24,12,384]{3,2,0,1:T(8,128)(2,1)S(1)}, u32[]{:S(2)}, u32[]{:S(2)}) async-start(bf16[3,24,12,384]{3,2,0,1:T(8,128)(2,1)} %copy.30), calls=%async_computation.1 | async-start | bytes 1769472 | tf_op jit(solution)/shard_map/all_to_all | solution.py:35
Sparse Core Ops, SparseCore 0:
  10.0 88.9 all-gather.4
  100.9 120.9 all-gather.2
where the time goes:
time: 338 us; the launch traced here: 335 us
  waiting for transfers between devices  221 us (65%)
  local copies, waits for them, and re-layouts  47.1 us (14%)
  blocking collectives  27.1 us (8%)
  matrix products  13.7 us (4%)
  between operations  13.5 us (4%)
  other arithmetic  6.46 us (2%)
  starting transfers between devices  6.17 us (2%)
    all_gather x1, waiting for transfers between devices, local(): lax.all_gather(amps_low, 'virt', axis=2, tiled=True)  123 us
    all_gather x1, waiting for transfers between devices, local(): columns = lax.all_gather(cycle_integrals, 'occ', axis=2, tiled=True)  86.2 us
    all_to_all x1, blocking collectives, local(): lax.all_to_all(partial_cycle.astype(jnp.bfloat16), 'virt', split_axis=3,...  27.1 us
    convert_element_type x2, local copies, waits for them, and re-layouts, local(): regrouped = lax.all_to_all(partial_cycle.astype(jnp.bfloat16), 'virt', sp...  24.1 us
    dot_general x1, matrix products, local(): jnp.einsum('ikac,bjkc->ibja', lax.all_gather(amps_low, 'virt', axis=2, ti...  13.7 us
    unnamed x6, local copies, waits for them, and re-layouts  12.9 us
    all_to_all x1, waiting for transfers between devices, local(): lax.all_to_all(direct.astype(jnp.bfloat16), 'occ', split_axis=1, concat_a...  11.4 us
  transfers between devices with their start and end apart: 3, of which 3 were waited for; matrix products, arithmetic and copies ran while one was open for 2% of the time, Pallas kernels for 0%

commit v1 on v0

v1 whole, which is shorter than its diff:
```python
import jax
import jax.numpy as jnp
from jax import lax
from jax.experimental import pallas as pl
from jax.experimental.pallas import tpu as pltpu
from jax.sharding import PartitionSpec as P

F32, BF16, I32 = jnp.float32, jnp.bfloat16, jnp.int32
MESH = pl.DeviceIdType.MESH
VMEM_LIMIT = 48 * 1024 * 1024


def iota(shape, dim):
    return lax.broadcasted_iota(I32, shape, dim)


def quot(x, d):
    s = 20
    return (x * (-(-(1 << s) // d))) >> s


def parts_of(x, d):
    q = quot(x, d)
    return q, x - q * d


def one_hot(mask):
    return jnp.where(mask, 1.0, 0.0).astype(BF16)


def pick(row, index):
    lanes = iota((index.shape[0], row.shape[1]), 1)
    return jnp.sum(jnp.where(lanes == index, row, 0.0), axis=1, keepdims=True)


def dot_nn(a, b):
    return lax.dot_general(a, b, (((1,), (0,)), ((), ())), preferred_element_type=F32)


def dot_nt(a, b):
    return lax.dot_general(a, b, (((1,), (1,)), ((), ())), preferred_element_type=F32)


def pack_kernel(amps, ints, occ_s, occ_r, virt_r, tsend, wsend, rank_out, rows):
    o, v = lax.axis_index("occ"), lax.axis_index("virt")
    y = lax.rem(o, 4)
    virt = virt_r[...]
    virtf = virt.astype(F32)
    occf = occ_r[...].astype(F32)
    r0, c0 = iota((384, 384), 0), iota((384, 384), 1)
    vcol = jnp.sum(jnp.where(r0 == c0, virtf, 0.0), axis=1, keepdims=True)
    rank = jnp.sum(jnp.where((vcol == virtf) & (r0 < c0), 1.0, 0.0), axis=0, keepdims=True)
    rank_out[...] = jnp.broadcast_to(rank, (8, 384))
    ranki = rank.astype(I32)

    b, j = parts_of(iota((288, 1), 0), 24)
    label = pick(virtf, v * 12 + b).astype(I32) ^ pick(occf, j).astype(I32)
    total = jnp.zeros((288, 384), F32)
    for k in range(3):
        w = ints[:, k].astype(F32).reshape(288, 384)
        w = jnp.where((label ^ occ_s[3 * o + k]) == virt, w, 0.0).astype(BF16)
        total += dot_nt(w, one_hot(r0 == ranki + (96 * k + 32 * y)))
    od, r = parts_of(iota((384, 1), 0), 48)
    jl, bb = r >> 4, r & 15
    source = jnp.where(bb < 12, bb * 24 + 3 * od + jl, -1)
    wsend[...] = dot_nn(one_hot(iota((384, 288), 1) == source), total.astype(BF16)).astype(BF16).reshape(8, 48, 384)

    ia, q = parts_of(iota((216, 1), 0), 6)
    i, a = parts_of(ia, 12)
    label = pick(virtf, v * 12 + a).astype(I32) ^ pick(occf, 3 * o + i).astype(I32)
    for lane in range(3):
        rows[lane] = amps[:, lane * 128 : lane * 128 + 128]
    total = jnp.zeros((216, 384), F32)
    for kk in range(4):
        t = jnp.concatenate([rows[lane, pl.ds(kk, 216, stride=4), :] for lane in range(3)], axis=1)
        t = jnp.where((label ^ pick(occf, 4 * q + kk).astype(I32)) == virt, t, 0.0).astype(BF16)
        total += dot_nt(t, one_hot(r0 == ranki + 96 * kk))
    qd, r = parts_of(iota((288, 1), 0), 48)
    il, aa = r >> 4, r & 15
    source = jnp.where(aa < 12, (il * 12 + aa) * 6 + qd, -1)
    t = dot_nn(one_hot(iota((288, 216), 1) == source), total.astype(BF16)).astype(BF16)
    for q in range(6):
        tsend[q // 3, :, (q % 3) * 384 : (q % 3 + 1) * 384] = t[q * 48 : (q + 1) * 48]


def cycle_kernel(
    tsend, wsend, occ_s, occ_r, virt_r, rank_r, resid,
    wstage, tbuf, wring, place, labels, rpart, rpeer, full, dsend, dbuf,
    w_send, w_recv, t_send, t_recv, ring_send, ring_recv, sib_send, sib_recv,
    r_send, r_recv, d_send, d_recv,
):
    o, v = lax.axis_index("occ"), lax.axis_index("virt")
    xh, y = o // 4, lax.rem(o, 4)
    z, s = v // 4, lax.rem(v, 4)
    xl, core = s // 2, lax.rem(s, 2)
    step = 1 - 2 * core
    znext = lax.rem(z + step + 8, 8)
    zback = lax.rem(z - step + 8, 8)

    barrier = pltpu.get_barrier_semaphore()
    for sd in range(4):
        def greet(d, _, sd=sd):
            pl.semaphore_signal(barrier, inc=1, device_id=(lax.rem(o + d, 8), z * 4 + lax.rem(s + sd, 4)), device_id_type=MESH)
            return 0
        lax.fori_loop(1 if sd == 0 else 0, 8, greet, 0)
    for zd in (znext, zback):
        pl.semaphore_signal(barrier, inc=1, device_id=(o, zd * 4 + s), device_id_type=MESH)
    pl.semaphore_wait(barrier, 33)

    def w_copy(d, c):
        od = lax.rem(o + d, 8)
        return pltpu.make_async_remote_copy(
            src_ref=wsend.at[od], dst_ref=wstage.at[y * 4 + s], send_sem=w_send, recv_sem=w_recv,
            device_id=(od, z * 4 + xh * 2 + c), device_id_type=MESH,
        )

    w_local = pltpu.make_async_copy(wsend.at[o], wstage.at[y * 4 + s], w_recv)
    for c in range(2):
        own = (xh == xl) & (core == c)

        @pl.when(own)
        def _():
            w_local.start()

        @pl.when(jnp.logical_not(own))
        def _(c=c):
            w_copy(0, c).start()

    def w_start(d, _):
        w_copy(d, 0).start()
        w_copy(d, 1).start()
        return 0

    lax.fori_loop(1, 8, w_start, 0)

    def t_copy(d, x):
        xd = lax.rem(xl + x, 2)
        return pltpu.make_async_remote_copy(
            src_ref=tsend.at[xd], dst_ref=tbuf.at[o, xl], send_sem=t_send, recv_sem=t_recv,
            device_id=(lax.rem(o + d, 8), z * 4 + xd * 2 + core), device_id_type=MESH,
        )

    t_local = pltpu.make_async_copy(tsend.at[xl], tbuf.at[o, xl], t_recv)
    t_local.start()
    t_copy(0, 1).start()

    def t_start(d, _):
        t_copy(d, 0).start()
        t_copy(d, 1).start()
        return 0

    lax.fori_loop(1, 8, t_start, 0)

    n = iota((1, 1152), 1)
    zz, r = parts_of(n, 144)
    jl, b48 = parts_of(r, 48)
    values = jnp.concatenate([rank_r[0:4, :], jnp.broadcast_to(virt_r[...].astype(F32), (4, 384))], axis=0)
    spread = dot_nn(values.astype(BF16), one_hot(iota((384, 1152), 0) == zz * 48 + b48)).astype(I32)
    place[...] = one_hot(iota((384, 1152), 0) == spread[0:1, :] + jl * 128)
    oj = jnp.where(jl == 0, occ_s[3 * o], jnp.where(jl == 1, occ_s[3 * o + 1], occ_s[3 * o + 2]))
    labels[...] = jnp.broadcast_to(spread[4:5, :] ^ oj, (8, 1152))

    row = iota((144, 1), 0)
    jr, br = parts_of(row, 48)
    sr, bl = parts_of(br, 12)
    gather = one_hot(iota((144, 192), 1) == sr * 48 + jr * 16 + bl)
    pltpu.make_async_copy(wstage, wstage, w_recv).wait()
    last = None
    for yy in range(4):
        piece = dot_nn(gather, wstage[yy * 4 : yy * 4 + 4].reshape(192, 384))
        first = piece[:, 0:128] if last is None else piece[:, 0:128] + last
        wring[z, :, yy * 256 : yy * 256 + 128] = first.astype(BF16)
        wring[z, :, yy * 256 + 128 : yy * 256 + 256] = piece[:, 128:256].astype(BF16)
        last = piece[:, 256:384]
    wring[z, :, 1024:1152] = last.astype(BF16)

    def ring_copy(t, rows):
        block = lax.rem(z - step * (t - 1) + 8, 8)
        return pltpu.make_async_remote_copy(
            src_ref=wring.at[block, rows], dst_ref=wring.at[block, rows],
            send_sem=ring_send.at[t - 1], recv_sem=ring_recv.at[t - 1],
            device_id=(o, znext * 4 + s), device_id_type=MESH,
        )

    def arrival(t, rows):
        block = lax.rem(z - step * t + 8, 8)
        return pltpu.make_async_copy(wring.at[block, rows], wring.at[block, rows], ring_recv.at[t - 1])

    def sib_copy(t, rows):
        block = lax.rem(z - step * t + 8, 8)
        return pltpu.make_async_remote_copy(
            src_ref=wring.at[block, rows], dst_ref=wring.at[block, rows],
            send_sem=sib_send.at[t - 1], recv_sem=sib_recv.at[t - 1],
            device_id=(o, z * 4 + xl * 2 + 1 - core), device_id_type=MESH,
        )

    def sib_arrival(t, rows):
        block = lax.rem(z + step * t + 8, 8)
        return pltpu.make_async_copy(wring.at[block, rows], wring.at[block, rows], sib_recv.at[t - 1])

    whole, lower, upper = pl.ds(0, 144), pl.ds(0, 80), pl.ds(80, 64)
    ring_copy(1, whole).start()
    for t in (1, 2):
        arrival(t, whole).wait()
        ring_copy(t + 1, whole).start()
        sib_copy(t, whole).start()
    arrival(3, whole).wait()
    for c, rows in ((0, lower), (1, upper)):
        @pl.when(core == c)
        def _(rows=rows):
            ring_copy(4, rows).start()
    sib_copy(3, whole).start()
    for c, rows, others in ((0, lower, upper), (1, upper, lower)):
        @pl.when(core == c)
        def _(rows=rows, others=others):
            arrival(4, rows).wait()
            sib_copy(4, rows).start()
            sib_arrival(4, others).wait()
    for t in (1, 2, 3):
        sib_arrival(t, whole).wait()

    pltpu.make_async_copy(tbuf, tbuf, t_recv).wait()

    virtf = virt_r[...].astype(F32)
    occf = occ_r[...].astype(F32)

    def r_copy(c):
        p = lax.rem(o // 2 + c, 4)
        return pltpu.make_async_remote_copy(
            src_ref=rpart.at[1 - xl, pl.ds(2 * p, 2)], dst_ref=rpeer.at[pl.ds(2 * p, 2)],
            send_sem=r_send.at[c], recv_sem=r_recv.at[c],
            device_id=(o, z * 4 + (1 - xl) * 2 + core), device_id_type=MESH,
        )

    def product(c, _):
        p = lax.rem(o // 2 + c, 4)
        left = tbuf[pl.ds(2 * p, 2)].reshape(192, 1152)
        block, r = parts_of(iota((192, 1), 0), 48)
        a = z * 48 + (block & 1) * 24 + core * 12 + (r & 15)
        i = 6 * p + 3 * (block >> 1) + (r >> 4)
        label = pick(virtf, a).astype(I32) ^ pick(occf, i).astype(I32)
        raw = dot_nt(left, wring[...].reshape(1152, 1152))
        raw = jnp.where(label == labels[0:1, :], raw, 0.0).astype(BF16)
        packed = dot_nt(raw, place[...]).astype(BF16)
        for u in range(2):
            for x in range(2):
                at = (u * 2 + x) * 48
                rpart[x, 2 * p + u] = packed[at : at + 48]
        r_copy(c).start()
        return 0

    lax.fori_loop(0, 4, product, 0)

    def d_copy(od):
        return pltpu.make_async_remote_copy(
            src_ref=dsend.at[od], dst_ref=dbuf.at[o], send_sem=d_send, recv_sem=d_recv,
            device_id=(od, v), device_id_type=MESH,
        )

    d_local = pltpu.make_async_copy(dsend.at[o], dbuf.at[o], d_recv)

    def combine(c, _):
        p = lax.rem(o // 2 + c, 4)
        r_copy(c).wait_recv()
        both = rpart[xl, pl.ds(2 * p, 2)].astype(F32) + rpeer[pl.ds(2 * p, 2)].astype(F32)
        full[pl.ds(2 * p, 2)] = both
        dsend[pl.ds(2 * p, 2)] = both.astype(BF16)
        for u in range(2):
            od = 2 * p + u

            @pl.when(od == o)
            def _():
                d_local.start()

            @pl.when(od != o)
            def _(od=od):
                d_copy(od).start()
        return 0

    lax.fori_loop(0, 4, combine, 0)
    pltpu.make_async_copy(dbuf, dbuf, d_recv).wait()

    def subtract(g, _):
        for i in range(3):
            for j in range(3):
                direct = dbuf[g, i * 16 : i * 16 + 16, j * 128 : j * 128 + 128].astype(F32)
                mirror = full[g, j * 16 : j * 16 + 16, i * 128 : i * 128 + 128]
                resid[g, i * 16 : i * 16 + 16, j * 128 : j * 128 + 128] = direct - mirror
        return 0

    lax.fori_loop(0, 8, subtract, 0)

    for c in range(2):
        @pl.when(jnp.logical_not((xh == xl) & (core == c)))
        def _(c=c):
            w_copy(0, c).wait_send()

    def sent(d, _):
        w_copy(d, 0).wait_send()
        w_copy(d, 1).wait_send()
        t_copy(d, 0).wait_send()
        t_copy(d, 1).wait_send()
        d_copy(lax.rem(o + d, 8)).wait_send()
        return 0

    lax.fori_loop(1, 8, sent, 0)
    t_copy(0, 1).wait_send()
    for t in (1, 2, 3):
        ring_copy(t, whole).wait_send()
        sib_copy(t, whole).wait_send()
    for c, rows in ((0, lower), (1, upper)):
        @pl.when(core == c)
        def _(rows=rows):
            ring_copy(4, rows).wait_send()
            sib_copy(4, rows).wait_send()
    for c in range(4):
        r_copy(c).wait_send()


def update_kernel(amps, resid, occ_r, virt_r, rank_r, occ_e, virt_e, out, spread):
    o, v = lax.axis_index("occ"), lax.axis_index("virt")
    virt = virt_r[...]
    occf, virtf = occ_r[...].astype(F32), virt.astype(F32)
    expand = one_hot(iota((128, 384), 0) == rank_r[0:1, :].astype(I32))
    for g in range(8):
        for jl in range(3):
            x = resid[g, :, jl * 128 : jl * 128 + 128]
            high = x.astype(BF16)
            low = (x - high.astype(F32)).astype(BF16)
            e = dot_nn(high, expand) + dot_nn(low, expand)
            for i in range(3):
                for lane in range(3):
                    spread[lane, pl.ds(i * 288 + 3 * g + jl, 12, stride=24), :] = e[i * 16 : i * 16 + 12, lane * 128 : lane * 128 + 128]
    for i in range(3):
        a, j = parts_of(iota((288, 1), 0), 24)
        at = pl.ds(i * 288, 288)
        label = pick(virtf, v * 12 + a).astype(I32) ^ pick(occf, j).astype(I32) ^ pick(occf, jnp.full((288, 1), 3 * o + i)).astype(I32)
        energy = pick(occ_e[...], jnp.full((288, 1), 3 * o + i)) + pick(occ_e[...], j) - pick(virt_e[...], v * 12 + a)
        denom = energy - virt_e[...]
        change = jnp.concatenate([spread[lane, at, :] for lane in range(3)], axis=1)
        out[at, :] = jnp.where(label == virt, amps[at, :] + change / denom, 0.0)


def local(amplitudes, cycle_integrals, occ_energy, virt_energy, occ_irrep, virt_irrep):
    vmem = pl.BlockSpec(memory_space=pltpu.VMEM)
    smem = pl.BlockSpec(memory_space=pltpu.SMEM)
    amps = jnp.transpose(amplitudes, (0, 2, 1, 3)).reshape(864, 384)
    ints = jnp.transpose(cycle_integrals, (0, 2, 1, 3))
    occ_r, virt_r = occ_irrep.reshape(1, 24), virt_irrep.reshape(1, 384)
    params = pltpu.CompilerParams(vmem_limit_bytes=VMEM_LIMIT)
    tsend, wsend, rank = pl.pallas_call(
        pack_kernel,
        out_shape=(
            jax.ShapeDtypeStruct((2, 48, 1152), BF16),
            jax.ShapeDtypeStruct((8, 48, 384), BF16),
            jax.ShapeDtypeStruct((8, 384), F32),
        ),
        in_specs=[vmem, vmem, smem, vmem, vmem],
        out_specs=(vmem, vmem, vmem),
        scratch_shapes=[pltpu.VMEM((3, 864, 128), F32)],
        compiler_params=params,
    )(amps, ints, occ_irrep, occ_r, virt_r)
    dma = pltpu.SemaphoreType.DMA
    resid = pl.pallas_call(
        cycle_kernel,
        out_shape=jax.ShapeDtypeStruct((8, 48, 384), F32),
        in_specs=[vmem, vmem, smem, vmem, vmem, vmem],
        out_specs=vmem,
        scratch_shapes=[
            pltpu.VMEM((16, 48, 384), BF16),
            pltpu.VMEM((8, 2, 48, 1152), BF16),
            pltpu.VMEM((8, 144, 1152), BF16),
            pltpu.VMEM((384, 1152), BF16),
            pltpu.VMEM((8, 1152), I32),
            pltpu.VMEM((2, 8, 48, 384), BF16),
            pltpu.VMEM((8, 48, 384), BF16),
            pltpu.VMEM((8, 48, 384), F32),
            pltpu.VMEM((8, 48, 384), BF16),
            pltpu.VMEM((8, 48, 384), BF16),
            dma, dma, dma, dma, dma((4,)), dma((4,)), dma((4,)), dma((4,)),
            dma((4,)), dma((4,)), dma, dma,
        ],
        compiler_params=pltpu.CompilerParams(
            collective_id=0, has_side_effects=True, vmem_limit_bytes=VMEM_LIMIT
        ),
    )(tsend, wsend, occ_irrep, occ_r, virt_r, rank)
    out = pl.pallas_call(
        update_kernel,
        out_shape=jax.ShapeDtypeStruct((864, 384), F32),
        in_specs=[vmem] * 7,
        out_specs=vmem,
        scratch_shapes=[pltpu.VMEM((3, 864, 128), F32)],
        compiler_params=params,
    )(amps, resid, occ_r, virt_r, rank, occ_energy.reshape(1, 24), virt_energy.reshape(1, 384))
    return jnp.transpose(out.reshape(3, 12, 24, 384), (0, 2, 1, 3))


def solution(mesh):
    return jax.shard_map(
        local,
        mesh=mesh,
        in_specs=(P("occ", None, "virt", None), P("virt", None, "occ", None), P(), P(), P(), P()),
        out_specs=P("occ", None, "virt", None),
        check_vma=False,
    )
```

time: 338 us -> 82.2 us (0.24)
  waiting for transfers between devices: 221 us -> 0 us
  Pallas kernels: 0 us -> 77.5 us
  local copies, waits for them, and re-layouts: 47.1 us -> 4.44 us
  blocking collectives: 27.1 us -> 0 us
  matrix products: 13.7 us -> 0 us
  between operations: 13.5 us -> 0.03 us
  other arithmetic: 6.46 us -> 0 us
  starting transfers between devices: 6.17 us -> 0 us
    all_gather x2 -> x0, waiting for transfers between devices: 209 us -> none  [the longest x1 123 us: local(): lax.all_gather(amps_low, 'virt', axis=2, tiled=True)]
    pallas_call x0 -> x3, Pallas kernels: none -> 77.5 us  [the longest x1 72.6 us: local(): pl.pallas_call(cycle_kernel, out_shape=jax.ShapeDtypeStruct((8, 48, 384),...]
    convert_element_type x4 -> x0, local copies, waits for them, and re-layouts: 29.5 us -> none  [the longest x2 24.1 us: local(): regrouped = lax.all_to_all(partial_cycle.astype(jnp.bfloat16), 'virt', sp...]
    all_to_all x1 -> x0, blocking collectives: 27.1 us -> none  [local(): lax.all_to_all(partial_cycle.astype(jnp.bfloat16), 'virt', split_axis=3,...]
    dot_general x1 -> x0, matrix products: 13.7 us -> none  [local(): jnp.einsum('ikac,bjkc->ibja', lax.all_gather(amps_low, 'virt', axis=2, ti...]
    all_to_all x1 -> x0, waiting for transfers between devices: 11.4 us -> none  [local(): lax.all_to_all(direct.astype(jnp.bfloat16), 'occ', split_axis=1, concat_a...]
    unnamed x6 -> x10, local copies, waits for them, and re-layouts: 12.9 us -> 3.07 us
    all_to_all x1 -> x0, starting transfers between devices: 6.13 us -> none  [local(): lax.all_to_all(direct.astype(jnp.bfloat16), 'occ', split_axis=1, concat_a...]
  transfers between devices with their start and end apart: 3 -> 0, of which waited for: 3 -> 0; matrix products, arithmetic and copies ran while one was open for 2% -> 0% of each run, Pallas kernels for 0% -> 0%
where the time goes in v1:
time: 82.2 us; the launch traced here: 82 us
  Pallas kernels  77.5 us (94%)
  local copies, waits for them, and re-layouts  4.44 us (5%)
    pallas_call x1, Pallas kernels, local(): pl.pallas_call(cycle_kernel, out_shape=jax.ShapeDtypeStruct((8, 48, 384),...  72.6 us
    unnamed x10, local copies, waits for them, and re-layouts  3.07 us
    pallas_call x1, Pallas kernels, local(): pl.pallas_call(update_kernel, out_shape=jax.ShapeDtypeStruct((864, 384),...  2.5 us
    pallas_call x1, Pallas kernels, local(): pl.pallas_call(pack_kernel, out_shape=(jax.ShapeDtypeStruct((2, 48, 1152)...  2.47 us

profile of v1, /device:TPU:1, one launch (start us, length us, event | category | flops | bytes accessed | tf_op | source)
XLA Modules:
  0.0 82.0 jit_solution(15837052940703445999)
XLA Ops:
  0.0 0.7 reshape.20.virt_r
  0.7 0.7 reshape.22.virt_e
  1.4 0.0 copy-start
  1.4 1.3 %copy-done = f32[3,24,12,384]{3,1,2,0:T(8,128)S(1)} copy-done((f32[3,24,12,384]{3,1,2,0:T(8,128)S(1)}, f32[3,24,12,384]{3,1,2,0:T(8,128)}, u32[]{:S(2)}) %copy-start) | copy-done | bytes 1327128
  2.7 0.0 copy-start.2
  2.7 1.1 %copy-done.2 = bf16[12,24,3,384]{3,1,2,0:T(8,128)(2,1)S(1)} copy-done((bf16[12,24,3,384]{3,1,2,0:T(8,128)(2,1)S(1)}, bf16[12,24,3,384]{3,1,2,0:T(8,128)(2,1)}, u32[]{:S(2)}) %copy-start.2) | copy-done | bytes 663576
  3.8 0.0 copy-start.3
  3.8 0.7 copy-done.3
  4.4 0.0 copy-start.1
  4.4 0.0 copy-start.4
  4.4 2.5 %shard_map.64 = (bf16[2,48,1152]{2,1,0:T(8,128)(2,1)S(1)}, bf16[8,48,384]{2,1,0:T(8,128)(2,1)S(1)}, f32[8,384]{1,0:T(8,128)S(1)}) custom-call(f32[864,384]{1,0:T(8,128)S(1)} %bitcast.9, bf16[12,3,24,384]{3,2,1,0:T(8,128)(2,1)S(1)} %bitcast.11, s32[24]{0:T(128)S(1)} %copy-done.3, s32[1,24]{1,0:T(1,128)S(1)} %bitcast.12, s32[1,384]{1,0:T(1,128)S(1)} %reshape.20.virt_r), custom_call_target="tpu_custom_call" | custom-call | tf_op jit(solution)/shard_map/pallas_call | solution.py:351
  6.9 72.6 %shard_map.65.resid = f32[8,48,384]{2,1,0:T(8,128)S(1)} custom-call(bf16[2,48,1152]{2,1,0:T(8,128)(2,1)S(1)} %get-tuple-element.8.tsend, bf16[8,48,384]{2,1,0:T(8,128)(2,1)S(1)} %get-tuple-element.9.wsend, s32[24]{0:T(128)S(1)} %copy-done.3, s32[1,24]{1,0:T(1,128)S(1)} %bitcast.13, s32[1,384]{1,0:T(1,128)S(1)} %reshape.20.virt_r, ...), custom_call_target="tpu_custom_call" | custom-call | tf_op jit(solution)/shard_map/pallas_call | solution.py:364
  79.5 0.0 copy-done.1
  79.5 0.0 copy-done.4
  79.5 2.5 %shard_map.66 = f32[864,384]{1,0:T(8,128)} custom-call(f32[864,384]{1,0:T(8,128)S(1)} %bitcast.10, f32[8,48,384]{2,1,0:T(8,128)S(1)} %shard_map.65.resid, s32[1,24]{1,0:T(1,128)S(1)} %bitcast.14, s32[1,384]{1,0:T(1,128)S(1)} %reshape.20.virt_r, f32[8,384]{1,0:T(8,128)S(1)} %get-tuple-element.10.rank_r, f32[1,24]{1,0:T(1,128)S(1)} %bitcast.15, ...), custom_call_target="tpu_custom_call" | custom-call | tf_op jit(solution)/shard_map/pallas_call | solution.py:387
Async XLA Ops:
  1.4 1.3 %copy-start = (f32[3,24,12,384]{3,1,2,0:T(8,128)S(1)}, f32[3,24,12,384]{3,1,2,0:T(8,128)}, u32[]{:S(2)}) copy-start(f32[3,24,12,384]{3,1,2,0:T(8,128)} %param.6) | copy-start | bytes 3981316
  2.7 1.1 %copy-start.2 = (bf16[12,24,3,384]{3,1,2,0:T(8,128)(2,1)S(1)}, bf16[12,24,3,384]{3,1,2,0:T(8,128)(2,1)}, u32[]{:S(2)}) copy-start(bf16[12,24,3,384]{3,1,2,0:T(8,128)(2,1)} %param.7) | copy-start | bytes 1990660
  3.8 0.7 copy-start.3
  4.4 75.1 %copy-start.1 = (f32[3,24,12,384]{3,1,2,0:T(8,128)S(1)}, f32[3,24,12,384]{3,1,2,0:T(8,128)}, u32[]{:S(2)}) copy-start(f32[3,24,12,384]{3,1,2,0:T(8,128)} %param.6) | copy-start | bytes 3981316
  4.4 75.1 %copy-start.4 = (f32[24]{0:T(128)S(1)}, f32[24]{0:T(128)}, u32[]{:S(2)}) copy-start(f32[24]{0:T(128)} %param.8) | copy-start | bytes 292

commit v2 on v1

--- a/solution.py
+++ b/solution.py
@@ -86,7 +86,7 @@
 def cycle_kernel(
     tsend, wsend, occ_s, occ_r, virt_r, rank_r, resid,
     wstage, tbuf, wring, place, labels, rpart, rpeer, full, dsend, dbuf,
-    w_send, w_recv, t_send, t_recv, ring_send, ring_recv, sib_send, sib_recv,
+    w_send, w_recv, ws_send, ws_recv, t_send, t_recv, ring_send, ring_recv, sib_send, sib_recv,
     r_send, r_recv, d_send, d_recv,
 ):
     o, v = lax.axis_index("occ"), lax.axis_index("virt")
@@ -107,28 +107,23 @@
         pl.semaphore_signal(barrier, inc=1, device_id=(o, zd * 4 + s), device_id_type=MESH)
     pl.semaphore_wait(barrier, 33)
 
-    def w_copy(d, c):
+    def w_copy(d):
         od = lax.rem(o + d, 8)
         return pltpu.make_async_remote_copy(
-            src_ref=wsend.at[od], dst_ref=wstage.at[y * 4 + s], send_sem=w_send, recv_sem=w_recv,
-            device_id=(od, z * 4 + xh * 2 + c), device_id_type=MESH,
-        )
-
-    w_local = pltpu.make_async_copy(wsend.at[o], wstage.at[y * 4 + s], w_recv)
-    for c in range(2):
-        own = (xh == xl) & (core == c)
-
-        @pl.when(own)
-        def _():
-            w_local.start()
-
-        @pl.when(jnp.logical_not(own))
-        def _(c=c):
-            w_copy(0, c).start()
+            src_ref=wsend.at[od], dst_ref=wstage.at[core, y * 2 + xl], send_sem=w_send, recv_sem=w_recv,
+            device_id=(od, z * 4 + xh * 2 + core), device_id_type=MESH,
+        )
+
+    @pl.when(xh == xl)
+    def _():
+        pltpu.make_async_copy(wsend.at[o], wstage.at[core, y * 2 + xl], w_recv).start()
+
+    @pl.when(xh != xl)
+    def _():
+        w_copy(0).start()
 
     def w_start(d, _):
-        w_copy(d, 0).start()
-        w_copy(d, 1).start()
+        w_copy(d).start()
         return 0
 
     lax.fori_loop(1, 8, w_start, 0)
@@ -163,61 +158,75 @@
     row = iota((144, 1), 0)
     jr, br = parts_of(row, 48)
     sr, bl = parts_of(br, 12)
-    gather = one_hot(iota((144, 192), 1) == sr * 48 + jr * 16 + bl)
-    pltpu.make_async_copy(wstage, wstage, w_recv).wait()
+    gather = one_hot(iota((144, 192), 1) == (sr & 1) * 96 + (sr >> 1) * 48 + jr * 16 + bl)
+    w_share = pltpu.make_async_remote_copy(
+        src_ref=wstage.at[core], dst_ref=wstage.at[core], send_sem=ws_send, recv_sem=ws_recv,
+        device_id=(o, z * 4 + xl * 2 + 1 - core), device_id_type=MESH,
+    )
+    pltpu.make_async_copy(wstage.at[core], wstage.at[core], w_recv).wait()
+    w_share.start()
+    pltpu.make_async_copy(wstage.at[1 - core], wstage.at[1 - core], ws_recv).wait()
     last = None
     for yy in range(4):
-        piece = dot_nn(gather, wstage[yy * 4 : yy * 4 + 4].reshape(192, 384))
+        piece = dot_nn(gather, wstage[:, yy * 2 : yy * 2 + 2].reshape(192, 384))
         first = piece[:, 0:128] if last is None else piece[:, 0:128] + last
         wring[z, :, yy * 256 : yy * 256 + 128] = first.astype(BF16)
         wring[z, :, yy * 256 + 128 : yy * 256 + 256] = piece[:, 128:256].astype(BF16)
         last = piece[:, 256:384]
     wring[z, :, 1024:1152] = last.astype(BF16)
 
-    def ring_copy(t, rows):
-        block = lax.rem(z - step * (t - 1) + 8, 8)
-        return pltpu.make_async_remote_copy(
-            src_ref=wring.at[block, rows], dst_ref=wring.at[block, rows],
-            send_sem=ring_send.at[t - 1], recv_sem=ring_recv.at[t - 1],
+    def piece_of(block, start, size):
+        return wring.at[lax.rem(block + 8, 8), pl.ds(pl.multiple_of(start, 16), size)]
+
+    def first_row(g, c):
+        return 48 * g + c * (96 - 96 * g)
+
+    def ring_copy(t, g, start, size=48):
+        ref = piece_of(z - step * (t - 1), start, size)
+        n = 3 * t - 3 + g
+        return pltpu.make_async_remote_copy(
+            src_ref=ref, dst_ref=ref, send_sem=ring_send.at[n], recv_sem=ring_recv.at[n],
             device_id=(o, znext * 4 + s), device_id_type=MESH,
         )
 
-    def arrival(t, rows):
-        block = lax.rem(z - step * t + 8, 8)
-        return pltpu.make_async_copy(wring.at[block, rows], wring.at[block, rows], ring_recv.at[t - 1])
-
-    def sib_copy(t, rows):
-        block = lax.rem(z - step * t + 8, 8)
-        return pltpu.make_async_remote_copy(
-            src_ref=wring.at[block, rows], dst_ref=wring.at[block, rows],
-            send_sem=sib_send.at[t - 1], recv_sem=sib_recv.at[t - 1],
+    def sib_copy(t, g, start, size=48):
+        ref = piece_of(z - step * t, start, size)
+        n = 3 * t - 3 + g
+        return pltpu.make_async_remote_copy(
+            src_ref=ref, dst_ref=ref, send_sem=sib_send.at[n], recv_sem=sib_recv.at[n],
             device_id=(o, z * 4 + xl * 2 + 1 - core), device_id_type=MESH,
         )
 
-    def sib_arrival(t, rows):
-        block = lax.rem(z + step * t + 8, 8)
-        return pltpu.make_async_copy(wring.at[block, rows], wring.at[block, rows], sib_recv.at[t - 1])
-
-    whole, lower, upper = pl.ds(0, 144), pl.ds(0, 80), pl.ds(80, 64)
-    ring_copy(1, whole).start()
-    for t in (1, 2):
-        arrival(t, whole).wait()
-        ring_copy(t + 1, whole).start()
-        sib_copy(t, whole).start()
-    arrival(3, whole).wait()
-    for c, rows in ((0, lower), (1, upper)):
+    def arrived(t, g, sems, way, start, size=48):
+        ref = piece_of(z - way * t, start, size)
+        pltpu.make_async_copy(ref, ref, sems.at[3 * t - 3 + g]).wait()
+
+    rest = ((48, 32), (80, 16))
+    for g in range(3):
+        ring_copy(1, g, first_row(g, core)).start()
+    for t in range(1, 4):
+        for g in range(3):
+            start = first_row(g, core)
+            arrived(t, g, ring_recv, step, start)
+            if t < 3 or g == 0:
+                ring_copy(t + 1, g, start).start()
+            elif g == 1:
+                for c in range(2):
+                    @pl.when(core == c)
+                    def _(c=c):
+                        ring_copy(4, 1, *rest[c]).start()
+            sib_copy(t, g, start).start()
+    arrived(4, 0, ring_recv, step, first_row(0, core))
+    sib_copy(4, 0, first_row(0, core)).start()
+    for c in range(2):
         @pl.when(core == c)
-        def _(rows=rows):
-            ring_copy(4, rows).start()
-    sib_copy(3, whole).start()
-    for c, rows, others in ((0, lower, upper), (1, upper, lower)):
-        @pl.when(core == c)
-        def _(rows=rows, others=others):
-            arrival(4, rows).wait()
-            sib_copy(4, rows).start()
-            sib_arrival(4, others).wait()
-    for t in (1, 2, 3):
-        sib_arrival(t, whole).wait()
+        def _(c=c):
+            arrived(4, 1, ring_recv, step, *rest[c])
+            sib_copy(4, 1, *rest[c]).start()
+            arrived(4, 1, sib_recv, -step, *rest[1 - c])
+    for t in range(1, 5):
+        for g in range(3 if t < 4 else 1):
+            arrived(t, g, sib_recv, -step, first_row(g, 1 - core))
 
     pltpu.make_async_copy(tbuf, tbuf, t_recv).wait()
 
@@ -290,14 +299,12 @@
 
     lax.fori_loop(0, 8, subtract, 0)
 
-    for c in range(2):
-        @pl.when(jnp.logical_not((xh == xl) & (core == c)))
-        def _(c=c):
-            w_copy(0, c).wait_send()
+    @pl.when(xh != xl)
+    def _():
+        w_copy(0).wait_send()
 
     def sent(d, _):
-        w_copy(d, 0).wait_send()
-        w_copy(d, 1).wait_send()
+        w_copy(d).wait_send()
         t_copy(d, 0).wait_send()
         t_copy(d, 1).wait_send()
         d_copy(lax.rem(o + d, 8)).wait_send()
@@ -305,14 +312,16 @@
 
     lax.fori_loop(1, 8, sent, 0)
     t_copy(0, 1).wait_send()
-    for t in (1, 2, 3):
-        ring_copy(t, whole).wait_send()
-        sib_copy(t, whole).wait_send()
-    for c, rows in ((0, lower), (1, upper)):
+    w_share.wait_send()
+    for t in range(1, 5):
+        for g in range(3 if t < 4 else 1):
+            ring_copy(t, g, first_row(g, core)).wait_send()
+            sib_copy(t, g, first_row(g, core)).wait_send()
+    for c in range(2):
         @pl.when(core == c)
-        def _(rows=rows):
-            ring_copy(4, rows).wait_send()
-            sib_copy(4, rows).wait_send()
+        def _(c=c):
+            ring_copy(4, 1, *rest[c]).wait_send()
+            sib_copy(4, 1, *rest[c]).wait_send()
     for c in range(4):
         r_copy(c).wait_send()
 
@@ -367,7 +376,7 @@
         in_specs=[vmem, vmem, smem, vmem, vmem, vmem],
         out_specs=vmem,
         scratch_shapes=[
-            pltpu.VMEM((16, 48, 384), BF16),
+            pltpu.VMEM((2, 8, 48, 384), BF16),
             pltpu.VMEM((8, 2, 48, 1152), BF16),
             pltpu.VMEM((8, 144, 1152), BF16),
             pltpu.VMEM((384, 1152), BF16),
@@ -377,7 +386,7 @@
             pltpu.VMEM((8, 48, 384), F32),
             pltpu.VMEM((8, 48, 384), BF16),
             pltpu.VMEM((8, 48, 384), BF16),
-            dma, dma, dma, dma, dma((4,)), dma((4,)), dma((4,)), dma((4,)),
+            dma, dma, dma, dma, dma, dma, dma((11,)), dma((11,)), dma((11,)), dma((11,)),
             dma((4,)), dma((4,)), dma, dma,
         ],
         compiler_params=pltpu.CompilerParams(

time: 82.2 us -> 68.5 us (0.83); the launches traced: 82 us -> 67.3 us
  Pallas kernels: 77.5 us -> 62.9 us
    pallas_call x1, Pallas kernels: 72.6 us -> 57.9 us  [local(): pl.pallas_call(cycle_kernel, out_shape=jax.ShapeDtypeStruct((8, 48, 384),...]
where the time goes in v2:
time: 68.5 us; the launch traced here: 67.3 us
  Pallas kernels  62.9 us (92%)
  local copies, waits for them, and re-layouts  4.44 us (6%)
    pallas_call x1, Pallas kernels, local(): pl.pallas_call(cycle_kernel, out_shape=jax.ShapeDtypeStruct((8, 48, 384),...  57.9 us
    unnamed x10, local copies, waits for them, and re-layouts  3.07 us
    pallas_call x1, Pallas kernels, local(): pl.pallas_call(update_kernel, out_shape=jax.ShapeDtypeStruct((864, 384),...  2.51 us
    pallas_call x1, Pallas kernels, local(): pl.pallas_call(pack_kernel, out_shape=(jax.ShapeDtypeStruct((2, 48, 1152)...  2.47 us

profile of v2, /device:TPU:1, one launch (start us, length us, event | category | flops | bytes accessed | tf_op | source)
XLA Modules:
  0.0 67.3 jit_solution(5937259208820009399)
XLA Ops:
  0.0 0.7 %reshape.20.virt_r = s32[1,384]{1,0:T(1,128)S(1)} reshape(s32[384]{0:T(512)} %param.11) | data formatting | bytes 3072 | tf_op jit(solution)/shard_map/reshape | solution.py:358
  0.7 0.7 %reshape.22.virt_e = f32[1,384]{1,0:T(1,128)S(1)} reshape(f32[384]{0:T(512)} %param.9) | data formatting | bytes 3072 | tf_op jit(solution)/shard_map/reshape | solution.py:403
  1.4 0.0 copy-start
  1.4 1.3 %copy-done = f32[3,24,12,384]{3,1,2,0:T(8,128)S(1)} copy-done((f32[3,24,12,384]{3,1,2,0:T(8,128)S(1)}, f32[3,24,12,384]{3,1,2,0:T(8,128)}, u32[]{:S(2)}) %copy-start) | copy-done | bytes 1327128
  2.7 0.0 copy-start.2
  2.7 1.1 %copy-done.2 = bf16[12,24,3,384]{3,1,2,0:T(8,128)(2,1)S(1)} copy-done((bf16[12,24,3,384]{3,1,2,0:T(8,128)(2,1)S(1)}, bf16[12,24,3,384]{3,1,2,0:T(8,128)(2,1)}, u32[]{:S(2)}) %copy-start.2) | copy-done | bytes 663576
  3.8 0.0 copy-start.3
  3.8 0.7 copy-done.3
  4.4 0.0 copy-start.1
  4.4 0.0 copy-start.4
  4.4 2.5 %shard_map.64 = (bf16[2,48,1152]{2,1,0:T(8,128)(2,1)S(1)}, bf16[8,48,384]{2,1,0:T(8,128)(2,1)S(1)}, f32[8,384]{1,0:T(8,128)S(1)}) custom-call(f32[864,384]{1,0:T(8,128)S(1)} %bitcast.9, bf16[12,3,24,384]{3,2,1,0:T(8,128)(2,1)S(1)} %bitcast.11, s32[24]{0:T(128)S(1)} %copy-done.3, s32[1,24]{1,0:T(1,128)S(1)} %bitcast.12, s32[1,384]{1,0:T(1,128)S(1)} %reshape.20.virt_r), custom_call_target="tpu_custom_call" | custom-call | tf_op jit(solution)/shard_map/pallas_call | solution.py:360
  6.9 57.9 %shard_map.65.resid = f32[8,48,384]{2,1,0:T(8,128)S(1)} custom-call(bf16[2,48,1152]{2,1,0:T(8,128)(2,1)S(1)} %get-tuple-element.8.tsend, bf16[8,48,384]{2,1,0:T(8,128)(2,1)S(1)} %get-tuple-element.9.wsend, s32[24]{0:T(128)S(1)} %copy-done.3, s32[1,24]{1,0:T(1,128)S(1)} %bitcast.13, s32[1,384]{1,0:T(1,128)S(1)} %reshape.20.virt_r, ...), custom_call_target="tpu_custom_call" | custom-call | tf_op jit(solution)/shard_map/pallas_call | solution.py:373
  64.8 0.0 copy-done.1
  64.8 0.0 copy-done.4
  64.8 2.5 %shard_map.66 = f32[864,384]{1,0:T(8,128)} custom-call(f32[864,384]{1,0:T(8,128)S(1)} %bitcast.10, f32[8,48,384]{2,1,0:T(8,128)S(1)} %shard_map.65.resid, s32[1,24]{1,0:T(1,128)S(1)} %bitcast.14, s32[1,384]{1,0:T(1,128)S(1)} %reshape.20.virt_r, f32[8,384]{1,0:T(8,128)S(1)} %get-tuple-element.10.rank_r, f32[1,24]{1,0:T(1,128)S(1)} %bitcast.15, ...), custom_call_target="tpu_custom_call" | custom-call | tf_op jit(solution)/shard_map/pallas_call | solution.py:396
Async XLA Ops:
  1.4 1.3 %copy-start = (f32[3,24,12,384]{3,1,2,0:T(8,128)S(1)}, f32[3,24,12,384]{3,1,2,0:T(8,128)}, u32[]{:S(2)}) copy-start(f32[3,24,12,384]{3,1,2,0:T(8,128)} %param.6) | copy-start | bytes 3981316
  2.7 1.1 %copy-start.2 = (bf16[12,24,3,384]{3,1,2,0:T(8,128)(2,1)S(1)}, bf16[12,24,3,384]{3,1,2,0:T(8,128)(2,1)}, u32[]{:S(2)}) copy-start(bf16[12,24,3,384]{3,1,2,0:T(8,128)(2,1)} %param.7) | copy-start | bytes 1990660
  3.8 0.7 copy-start.3
  4.4 60.4 %copy-start.1 = (f32[3,24,12,384]{3,1,2,0:T(8,128)S(1)}, f32[3,24,12,384]{3,1,2,0:T(8,128)}, u32[]{:S(2)}) copy-start(f32[3,24,12,384]{3,1,2,0:T(8,128)} %param.6) | copy-start | bytes 3981316
  4.4 60.4 %copy-start.4 = (f32[24]{0:T(128)S(1)}, f32[24]{0:T(128)}, u32[]{:S(2)}) copy-start(f32[24]{0:T(128)} %param.8) | copy-start | bytes 292

commit v3 on v2

v3 whole, which is shorter than its diff:
```python
import jax
import jax.numpy as jnp
from jax import lax
from jax.experimental import pallas as pl
from jax.experimental.pallas import tpu as pltpu
from jax.sharding import PartitionSpec as P

F32, BF16, I32 = jnp.float32, jnp.bfloat16, jnp.int32
MESH = pl.DeviceIdType.MESH
VMEM_LIMIT = 60 << 20


def iota(shape, dim):
    return lax.broadcasted_iota(I32, shape, dim)


def quot(x, d):
    s = 20
    return (x * (-(-(1 << s) // d))) >> s


def parts_of(x, d):
    q = quot(x, d)
    return q, x - q * d


def one_hot(mask):
    return jnp.where(mask, 1.0, 0.0).astype(BF16)


def pick(row, index):
    lanes = iota((index.shape[0], row.shape[1]), 1)
    return jnp.sum(jnp.where(lanes == index, row, 0.0), axis=1, keepdims=True)


def dot_nn(a, b):
    return lax.dot_general(a, b, (((1,), (0,)), ((), ())), preferred_element_type=F32)


def dot_nt(a, b):
    return lax.dot_general(a, b, (((1,), (1,)), ((), ())), preferred_element_type=F32)


def cycle_kernel(
    amps_h, ints_h, occ_s, occ_h, virt_h, occ_eh, virt_eh, out,
    occ_r, virt_r, occ_e, virt_e, gain, expand, diff, amps, ints, rows, tsend, wsend, wstage, tbuf, wring, place, labels, last_rows, gather_last, to_rows, to_owner, rpart, rpeer, dsend, dbuf,
    w_send, w_recv, ws_send, ws_recv, t_send, t_recv, ring_send, ring_recv, sib_send, sib_recv,
    r_send, r_recv, d_send, d_recv, in_sems,
):
    load_ints = pltpu.make_async_copy(ints_h, ints, in_sems.at[0])
    load_amps = pltpu.make_async_copy(amps_h, amps, in_sems.at[1])
    loads = [
        pltpu.make_async_copy(src, dst, in_sems.at[n + 2])
        for n, (src, dst) in enumerate([(occ_h, occ_r), (virt_h, virt_r), (occ_eh, occ_e), (virt_eh, virt_e)])
    ]
    for load in loads:
        load.start()
    load_ints.start()
    load_amps.start()
    o, v = lax.axis_index("occ"), lax.axis_index("virt")
    xh, y = o // 4, lax.rem(o, 4)
    z, s = v // 4, lax.rem(v, 4)
    xl, core = s // 2, lax.rem(s, 2)
    step = 1 - 2 * core
    znext = lax.rem(z + step + 8, 8)
    zback = lax.rem(z - step + 8, 8)

    barrier = pltpu.get_barrier_semaphore()
    for sd in range(4):
        def greet(d, _, sd=sd):
            pl.semaphore_signal(barrier, inc=1, device_id=(lax.rem(o + d, 8), z * 4 + lax.rem(s + sd, 4)), device_id_type=MESH)
            return 0
        lax.fori_loop(1 if sd == 0 else 0, 8, greet, 0)
    for zd in (znext, zback):
        pl.semaphore_signal(barrier, inc=1, device_id=(o, zd * 4 + s), device_id_type=MESH)

    for load in loads:
        load.wait()
    virt = virt_r[...].reshape(1, 384)
    virtf = virt.astype(F32)
    occf = occ_r[...].reshape(1, 24).astype(F32)
    r0, c0 = iota((384, 384), 0), iota((384, 384), 1)
    vcol = jnp.sum(jnp.where(r0 == c0, virtf, 0.0), axis=1, keepdims=True)
    rank = jnp.sum(jnp.where((vcol == virtf) & (r0 < c0), 1.0, 0.0), axis=0, keepdims=True)
    ranki = rank.astype(I32)

    load_ints.wait()
    b, j = parts_of(iota((288, 1), 0), 24)
    label = pick(virtf, v * 12 + b).astype(I32) ^ pick(occf, j).astype(I32)
    total = jnp.zeros((288, 384), F32)
    for k in range(3):
        w = ints[:, k].astype(F32).reshape(288, 384)
        w = jnp.where((label ^ occ_s[3 * o + k]) == virt, w, 0.0).astype(BF16)
        total += dot_nt(w, one_hot(r0 == ranki + (96 * k + 32 * y)))
    od, r = parts_of(iota((384, 1), 0), 48)
    jl, bb = r >> 4, r & 15
    source = jnp.where(bb < 12, bb * 24 + 3 * od + jl, -1)
    wsend[...] = dot_nn(one_hot(iota((384, 288), 1) == source), total.astype(BF16)).astype(BF16).reshape(8, 48, 384)

    pl.semaphore_wait(barrier, 33)

    def w_copy(d):
        od = lax.rem(o + d, 8)
        return pltpu.make_async_remote_copy(
            src_ref=wsend.at[od], dst_ref=wstage.at[core, y * 2 + xl], send_sem=w_send, recv_sem=w_recv,
            device_id=(od, z * 4 + xh * 2 + core), device_id_type=MESH,
        )

    @pl.when(xh == xl)
    def _():
        pltpu.make_async_copy(wsend.at[o], wstage.at[core, y * 2 + xl], w_recv).start()

    @pl.when(xh != xl)
    def _():
        w_copy(0).start()

    def w_start(d, _):
        w_copy(d).start()
        return 0

    lax.fori_loop(1, 8, w_start, 0)

    def t_copy(d, x):
        xd = lax.rem(xl + x, 2)
        return pltpu.make_async_remote_copy(
            src_ref=tsend.at[xd], dst_ref=tbuf.at[o, xl], send_sem=t_send, recv_sem=t_recv,
            device_id=(lax.rem(o + d, 8), z * 4 + xd * 2 + core), device_id_type=MESH,
        )

    load_amps.wait()
    ia, q = parts_of(iota((216, 1), 0), 6)
    i, a = parts_of(ia, 12)
    label = pick(virtf, v * 12 + a).astype(I32) ^ pick(occf, 3 * o + i).astype(I32)
    for lane in range(3):
        rows[lane] = amps[:, lane * 128 : lane * 128 + 128]
    total = jnp.zeros((216, 384), F32)
    for kk in range(4):
        t = jnp.concatenate([rows[lane, pl.ds(kk, 216, stride=4), :] for lane in range(3)], axis=1)
        t = jnp.where((label ^ pick(occf, 4 * q + kk).astype(I32)) == virt, t, 0.0).astype(BF16)
        total += dot_nt(t, one_hot(r0 == ranki + 96 * kk))
    qd, r = parts_of(iota((288, 1), 0), 48)
    source = jnp.where(r < 36, r * 6 + qd, -1)
    t = dot_nn(one_hot(iota((288, 216), 1) == source), total.astype(BF16))
    last_rows[...] = jnp.zeros((2, 48, 128), F32)
    for q in range(6):
        for lane in range(3):
            tile = t[q * 48 : q * 48 + 36, lane * 128 : lane * 128 + 128]
            n = (q % 3) * 3 + lane
            tsend[q // 3, n * 32 : n * 32 + 32] = tile[0:32].astype(BF16)
            last_rows[q // 3, n * 4 : n * 4 + 4] = tile[32:36]
    tsend[:, 288:336] = last_rows[...].astype(BF16)

    n = iota((144, 1), 0)
    gather_last[...] = one_hot(iota((144, 192), 1) == ((n & 15) >> 2) * 48 + (n >> 4) * 4 + (n & 3))
    n = iota((160, 1), 0)
    x, n = parts_of(n, 80)
    u, r = parts_of(n, 36)
    block = u * 2 + x
    source = jnp.where(u < 2, jnp.where(r < 32, block * 32 + r, 96 + block * 4 + r), -1)
    to_rows[...] = one_hot(iota((160, 144), 1) == source)
    u, r = parts_of(iota((96, 1), 0), 48)
    i, a = r >> 4, r & 15
    to_owner[...] = one_hot(iota((96, 80), 1) == jnp.where(a < 12, u * 36 + i * 12 + a, -1))

    n = iota((1, 1152), 1)
    zz, r = parts_of(n, 144)
    jl, b48 = parts_of(r, 48)
    values = jnp.concatenate([jnp.broadcast_to(rank, (4, 384)), jnp.broadcast_to(virtf, (4, 384))], axis=0)
    spread = dot_nn(values.astype(BF16), one_hot(iota((384, 1152), 0) == zz * 48 + b48)).astype(I32)
    place[...] = one_hot(iota((384, 1152), 0) == spread[0:1, :] + jl * 128)
    oj = jnp.where(jl == 0, occ_s[3 * o], jnp.where(jl == 1, occ_s[3 * o + 1], occ_s[3 * o + 2]))
    labels[...] = jnp.broadcast_to(spread[4:5, :] ^ oj, (8, 1152))

    row = iota((144, 1), 0)
    jr, br = parts_of(row, 48)
    sr, bl = parts_of(br, 12)
    gather = one_hot(iota((144, 192), 1) == (sr & 1) * 96 + (sr >> 1) * 48 + jr * 16 + bl)
    w_share = pltpu.make_async_remote_copy(
        src_ref=wstage.at[core], dst_ref=wstage.at[core], send_sem=ws_send, recv_sem=ws_recv,
        device_id=(o, z * 4 + xl * 2 + 1 - core), device_id_type=MESH,
    )
    pltpu.make_async_copy(wstage.at[core], wstage.at[core], w_recv).wait()
    w_share.start()
    pltpu.make_async_copy(tsend.at[xl], tbuf.at[o, xl], t_recv).start()
    for n in range(15):
        t_copy((n + 1) // 2, (n + 1) % 2).start()
    pltpu.make_async_copy(wstage.at[1 - core], wstage.at[1 - core], ws_recv).wait()
    last = None
    for yy in range(4):
        piece = dot_nn(gather, wstage[:, yy * 2 : yy * 2 + 2].reshape(192, 384))
        first = piece[:, 0:128] if last is None else piece[:, 0:128] + last
        wring[z, :, yy * 256 : yy * 256 + 128] = first.astype(BF16)
        wring[z, :, yy * 256 + 128 : yy * 256 + 256] = piece[:, 128:256].astype(BF16)
        last = piece[:, 256:384]
    wring[z, :, 1024:1152] = last.astype(BF16)

    def piece_of(block, start, size):
        return wring.at[lax.rem(block + 8, 8), pl.ds(pl.multiple_of(start, 16), size)]

    def first_row(g, c):
        return 48 * g + c * (96 - 96 * g)

    def ring_copy(t, g, start, size=48):
        ref = piece_of(z - step * (t - 1), start, size)
        n = 3 * t - 3 + g
        return pltpu.make_async_remote_copy(
            src_ref=ref, dst_ref=ref, send_sem=ring_send.at[n], recv_sem=ring_recv.at[n],
            device_id=(o, znext * 4 + s), device_id_type=MESH,
        )

    def sib_copy(t, g, start, size=48):
        ref = piece_of(z - step * t, start, size)
        n = 3 * t - 3 + g
        return pltpu.make_async_remote_copy(
            src_ref=ref, dst_ref=ref, send_sem=sib_send.at[n], recv_sem=sib_recv.at[n],
            device_id=(o, z * 4 + xl * 2 + 1 - core), device_id_type=MESH,
        )

    def arrived(t, g, sems, way, start, size=48):
        ref = piece_of(z - way * t, start, size)
        pltpu.make_async_copy(ref, ref, sems.at[3 * t - 3 + g]).wait()

    rest = ((48, 32), (80, 16))
    for g in range(3):
        ring_copy(1, g, first_row(g, core)).start()

    expand[...] = one_hot((iota((256, 384), 0) & 127) == ranki)
    occ_en, virt_en = occ_e[...].reshape(1, 24), virt_e[...].reshape(1, 384)
    for i in range(3):
        a, j = parts_of(iota((288, 1), 0), 24)
        at = pl.ds(i * 288, 288)
        own = jnp.full((288, 1), 3 * o + i)
        label = pick(virtf, v * 12 + a).astype(I32) ^ pick(occf, j).astype(I32) ^ pick(occf, own).astype(I32)
        denom = pick(occ_en, own) + pick(occ_en, j) - pick(virt_en, v * 12 + a) - virt_en
        gain[at, :] = jnp.where(label == virt, 1.0 / denom, 0.0)
        amps[at, :] = jnp.where(label == virt, amps[at, :], 0.0)

    for t in range(1, 4):
        for g in range(3):
            start = first_row(g, core)
            arrived(t, g, ring_recv, step, start)
            if t < 3 or g == 0:
                ring_copy(t + 1, g, start).start()
            elif g == 1:
                for c in range(2):
                    @pl.when(core == c)
                    def _(c=c):
                        ring_copy(4, 1, *rest[c]).start()
            sib_copy(t, g, start).start()
    arrived(4, 0, ring_recv, step, first_row(0, core))
    sib_copy(4, 0, first_row(0, core)).start()
    for c in range(2):
        @pl.when(core == c)
        def _(c=c):
            arrived(4, 1, ring_recv, step, *rest[c])
            sib_copy(4, 1, *rest[c]).start()
            arrived(4, 1, sib_recv, -step, *rest[1 - c])
    for t in range(1, 5):
        for g in range(3 if t < 4 else 1):
            arrived(t, g, sib_recv, -step, first_row(g, 1 - core))

    pltpu.make_async_copy(tbuf, tbuf, t_recv).wait()


    def r_copy(c):
        p = lax.rem(o // 2 + c, 4)
        return pltpu.make_async_remote_copy(
            src_ref=rpart.at[1 - xl, p], dst_ref=rpeer.at[p],
            send_sem=r_send.at[c], recv_sem=r_recv.at[c],
            device_id=(o, z * 4 + (1 - xl) * 2 + core), device_id_type=MESH,
        )

    def product(c, _):
        p = lax.rem(o // 2 + c, 4)
        tiles = tbuf[pl.ds(2 * p, 2)].reshape(4, 336, 128)
        last = dot_nn(gather_last[...], tiles[:, 288:336].reshape(192, 128)).astype(BF16)
        left = jnp.concatenate(
            [
                jnp.concatenate([tiles[:, n * 32 : n * 32 + 32].reshape(128, 128), last[n * 16 : n * 16 + 16]], axis=0)
                for n in range(9)
            ],
            axis=1,
        )
        n = iota((144, 1), 0)
        block = jnp.where(n < 128, n >> 5, (n - 128) >> 2)
        il, a = parts_of(jnp.where(n < 128, n & 31, 32 + (n & 3)), 12)
        a = z * 48 + (block & 1) * 24 + core * 12 + a
        i = 6 * p + 3 * (block >> 1) + il
        label = pick(virtf, a).astype(I32) ^ pick(occf, i).astype(I32)
        raw = dot_nt(left, wring[...].reshape(1152, 1152))
        raw = jnp.where(label == labels[0:1, :], raw, 0.0).astype(BF16)
        packed = dot_nn(to_rows[...], dot_nt(raw, place[...]).astype(BF16)).astype(BF16)
        rpart[0, p] = packed[0:80]
        rpart[1, p] = packed[80:160]
        r_copy(c).start()
        return 0

    lax.fori_loop(0, 4, product, 0)

    def d_copy(od):
        return pltpu.make_async_remote_copy(
            src_ref=dsend.at[od], dst_ref=dbuf.at[o], send_sem=d_send, recv_sem=d_recv,
            device_id=(od, v), device_id_type=MESH,
        )

    d_local = pltpu.make_async_copy(dsend.at[o], dbuf.at[o], d_recv)

    def combine(c, _):
        p = lax.rem(o // 2 + c, 4)
        r_copy(c).wait_recv()
        both = rpart[xl, p].astype(F32) + rpeer[p].astype(F32)
        dsend[pl.ds(2 * p, 2)] = dot_nn(to_owner[...], both.astype(BF16)).astype(BF16).reshape(2, 48, 384)
        for u in range(2):
            od = 2 * p + u

            @pl.when(od == o)
            def _():
                d_local.start()

            @pl.when(od != o)
            def _(od=od):
                d_copy(od).start()
        return 0

    lax.fori_loop(0, 4, combine, 0)
    pltpu.make_async_copy(dbuf, dbuf, d_recv).wait()

    def differ(g, _):
        for jl in range(3):
            direct = dbuf[g, :, jl * 128 : jl * 128 + 128].astype(F32)
            for i in range(3):
                change = direct[i * 16 : i * 16 + 16] - dsend[g, jl * 16 : jl * 16 + 16, i * 128 : i * 128 + 128].astype(F32)
                high = change.astype(BF16)
                diff[i, 3 * g + jl, :, 0:128] = high
                diff[i, 3 * g + jl, :, 128:256] = (change - high.astype(F32)).astype(BF16)
        return 0

    lax.fori_loop(0, 8, differ, 0)
    stores = []
    for i in range(3):
        at = pl.ds(i * 288, 288)
        e = dot_nn(diff[i].reshape(384, 256), expand[...])
        for j in range(24):
            for lane in range(3):
                rows[lane, pl.ds(i * 288 + j, 12, stride=24), :] = e[j * 16 : j * 16 + 12, lane * 128 : lane * 128 + 128]
        for lane in range(3):
            to = slice(lane * 128, lane * 128 + 128)
            amps[at, to] = amps[at, to] + rows[lane, at, :] * gain[at, to]
        stores.append(pltpu.make_async_copy(amps.at[at], out.at[at], in_sems.at[i]))
        stores[i].start()

    @pl.when(xh != xl)
    def _():
        w_copy(0).wait_send()

    def sent(d, _):
        w_copy(d).wait_send()
        t_copy(d, 0).wait_send()
        t_copy(d, 1).wait_send()
        d_copy(lax.rem(o + d, 8)).wait_send()
        return 0

    lax.fori_loop(1, 8, sent, 0)
    t_copy(0, 1).wait_send()
    w_share.wait_send()
    for t in range(1, 5):
        for g in range(3 if t < 4 else 1):
            ring_copy(t, g, first_row(g, core)).wait_send()
            sib_copy(t, g, first_row(g, core)).wait_send()
    for c in range(2):
        @pl.when(core == c)
        def _(c=c):
            ring_copy(4, 1, *rest[c]).wait_send()
            sib_copy(4, 1, *rest[c]).wait_send()
    for c in range(4):
        r_copy(c).wait_send()
    for store in stores:
        store.wait()


def local(amplitudes, cycle_integrals, occ_energy, virt_energy, occ_irrep, virt_irrep):
    smem = pl.BlockSpec(memory_space=pltpu.SMEM)
    amps = jnp.transpose(amplitudes, (0, 2, 1, 3)).reshape(864, 384)
    ints = jnp.transpose(cycle_integrals, (0, 2, 1, 3))
    dma = pltpu.SemaphoreType.DMA
    hbm = pl.BlockSpec(memory_space=pltpu.HBM)
    out = pl.pallas_call(
        cycle_kernel,
        out_shape=jax.ShapeDtypeStruct((864, 384), F32),
        in_specs=[hbm, hbm, smem, hbm, hbm, hbm, hbm],
        out_specs=hbm,
        scratch_shapes=[
            pltpu.VMEM((24,), I32),
            pltpu.VMEM((384,), I32),
            pltpu.VMEM((24,), F32),
            pltpu.VMEM((384,), F32),
            pltpu.VMEM((864, 384), F32),
            pltpu.VMEM((256, 384), BF16),
            pltpu.VMEM((3, 24, 16, 256), BF16),
            pltpu.VMEM((864, 384), F32),
            pltpu.VMEM((12, 3, 24, 384), BF16),
            pltpu.VMEM((3, 864, 128), F32),
            pltpu.VMEM((2, 336, 128), BF16),
            pltpu.VMEM((8, 48, 384), BF16),
            pltpu.VMEM((2, 8, 48, 384), BF16),
            pltpu.VMEM((8, 2, 336, 128), BF16),
            pltpu.VMEM((8, 144, 1152), BF16),
            pltpu.VMEM((384, 1152), BF16),
            pltpu.VMEM((8, 1152), I32),
            pltpu.VMEM((2, 48, 128), F32),
            pltpu.VMEM((144, 192), BF16),
            pltpu.VMEM((160, 144), BF16),
            pltpu.VMEM((96, 80), BF16),
            pltpu.VMEM((2, 4, 80, 384), BF16),
            pltpu.VMEM((4, 80, 384), BF16),
            pltpu.VMEM((8, 48, 384), BF16),
            pltpu.VMEM((8, 48, 384), BF16),
            dma, dma, dma, dma, dma, dma, dma((11,)), dma((11,)), dma((11,)), dma((11,)),
            dma((4,)), dma((4,)), dma, dma, dma((6,)),
        ],
        compiler_params=pltpu.CompilerParams(
            collective_id=0, has_side_effects=True, vmem_limit_bytes=VMEM_LIMIT
        ),
    )(amps, ints, occ_irrep, occ_irrep, virt_irrep, occ_energy, virt_energy)
    return jnp.transpose(out.reshape(3, 12, 24, 384), (0, 2, 1, 3))


def solution(mesh):
    return jax.shard_map(
        local,
        mesh=mesh,
        in_specs=(P("occ", None, "virt", None), P("virt", None, "occ", None), P(), P(), P(), P()),
        out_specs=P("occ", None, "virt", None),
        check_vma=False,
    )
```

time: 68.5 us -> 57.4 us (0.84); the launches traced: 67.3 us -> 57.2 us
  Pallas kernels: 62.9 us -> 54.8 us
  local copies, waits for them, and re-layouts: 4.44 us -> 2.47 us
    pallas_call x3 -> x1, Pallas kernels: 62.9 us -> 54.8 us  [local(): pl.pallas_call(cycle_kernel, out_shape=jax.ShapeDtypeStruct((864, 384), F...]
    reshape x2 -> x0, local copies, waits for them, and re-layouts: 1.37 us -> none  [the longest x1 0.68 us: local(): occ_r, virt_r = (occ_irrep.reshape(1, 24), virt_irrep.reshape(1, 384))]
    unnamed x10 -> x1, local copies, waits for them, and re-layouts: 3.07 us -> 2.47 us
where the time goes in v3:
time: 57.4 us; the launch traced here: 57.2 us
  Pallas kernels  54.8 us (95%)
  local copies, waits for them, and re-layouts  2.47 us (4%)
    pallas_call x1, Pallas kernels, local(): pl.pallas_call(cycle_kernel, out_shape=jax.ShapeDtypeStruct((864, 384), F...  54.8 us
    unnamed x1, local copies, waits for them, and re-layouts  2.47 us

profile of v3, /device:TPU:1, one launch (start us, length us, event | category | flops | bytes accessed | tf_op | source)
XLA Modules:
  0.0 57.2 jit_solution(1820391886391133599)
XLA Ops:
  0.0 54.8 %shard_map.64 = f32[864,384]{1,0:T(8,128)} custom-call(f32[864,384]{1,0:T(8,128)} %bitcast.8, bf16[12,3,24,384]{3,2,1,0:T(8,128)(2,1)} %bitcast.9, s32[24]{0:T(128)} %occ_h.1, s32[24]{0:T(128)} %occ_h.1, s32[384]{0:T(512)} %virt_h.1, f32[24]{0:T(128)} %occ_eh.1, f32[384]{0:T(512)} %virt_eh.1), custom_call_target="tpu_custom_call" | custom-call | tf_op jit(solution)/shard_map/pallas_call | solution.py:387
  54.8 2.5 %copy.8 = f32[3,24,12,384]{3,1,2,0:T(8,128)} copy(f32[3,24,12,384]{3,1,2,0:T(8,128)} %bitcast.7) | data formatting | bytes 2654208

commit v4 on v3

v4 whole, which is shorter than its diff:
```python
import jax
import jax.numpy as jnp
from jax import lax
from jax.experimental import pallas as pl
from jax.experimental.pallas import tpu as pltpu
from jax.sharding import PartitionSpec as P

F32, BF16, I32 = jnp.float32, jnp.bfloat16, jnp.int32
MESH = pl.DeviceIdType.MESH
VMEM_LIMIT = 60 << 20


def iota(shape, dim):
    return lax.broadcasted_iota(I32, shape, dim)


def quot(x, d):
    s = 20
    return (x * (-(-(1 << s) // d))) >> s


def parts_of(x, d):
    q = quot(x, d)
    return q, x - q * d


def one_hot(mask):
    return jnp.where(mask, 1.0, 0.0).astype(BF16)


def pick(row, index):
    lanes = iota((index.shape[0], row.shape[1]), 1)
    return jnp.sum(jnp.where(lanes == index, row, 0.0), axis=1, keepdims=True)


def dot_nn(a, b):
    return lax.dot_general(a, b, (((1,), (0,)), ((), ())), preferred_element_type=F32)


def dot_nt(a, b):
    return lax.dot_general(a, b, (((1,), (1,)), ((), ())), preferred_element_type=F32)


def cycle_kernel(
    amps_h, ints_h, occ_s, occ_h, virt_h, occ_eh, virt_eh, out,
    occ_r, virt_r, occ_e, virt_e, gain, expand, diff, amps, ints, rows, tsend, w_last, wsend, wstage, tbuf, wring, place, labels, last_rows, gather_last, to_rows, to_owner, row_labels,
    left, rpart, rpeer, dsend, dbuf,
    w_send, w_recv, t_send, t_recv, ring_send, ring_recv, sib_send, sib_recv,
    r_send, r_recv, d_send, d_recv, in_sems,
):
    load_ints = pltpu.make_async_copy(ints_h, ints, in_sems.at[0])
    load_amps = pltpu.make_async_copy(amps_h, amps, in_sems.at[1])
    loads = [
        pltpu.make_async_copy(src, dst, in_sems.at[n + 2])
        for n, (src, dst) in enumerate([(occ_h, occ_r), (virt_h, virt_r), (occ_eh, occ_e), (virt_eh, virt_e)])
    ]
    for load in loads:
        load.start()
    load_ints.start()
    load_amps.start()
    o, v = lax.axis_index("occ"), lax.axis_index("virt")
    xh, y = o // 4, lax.rem(o, 4)
    z, s = v // 4, lax.rem(v, 4)
    xl, core = s // 2, lax.rem(s, 2)

    barrier = pltpu.get_barrier_semaphore()
    for sd in range(4):
        def greet(d, _, sd=sd):
            pl.semaphore_signal(barrier, inc=1, device_id=(lax.rem(o + d, 8), z * 4 + lax.rem(s + sd, 4)), device_id_type=MESH)
            return 0
        lax.fori_loop(1 if sd == 0 else 0, 8, greet, 0)
    for zd in (lax.rem(z + 1, 8), lax.rem(z + 7, 8)):
        pl.semaphore_signal(barrier, inc=1, device_id=(o, zd * 4 + s), device_id_type=MESH)

    for load in loads:
        load.wait()
    virt = virt_r[...].reshape(1, 384)
    virtf = virt.astype(F32)
    occf = occ_r[...].reshape(1, 24).astype(F32)
    r0, c0 = iota((384, 384), 0), iota((384, 384), 1)
    vcol = jnp.sum(jnp.where(r0 == c0, virtf, 0.0), axis=1, keepdims=True)
    rank = jnp.sum(jnp.where((vcol == virtf) & (r0 < c0), 1.0, 0.0), axis=0, keepdims=True)
    ranki = rank.astype(I32)

    load_ints.wait()
    b, j = parts_of(iota((288, 1), 0), 24)
    label = pick(virtf, v * 12 + b).astype(I32) ^ pick(occf, j).astype(I32)
    total = jnp.zeros((288, 384), F32)
    for k in range(3):
        w = ints[:, k].astype(F32).reshape(288, 384)
        w = jnp.where((label ^ occ_s[3 * o + k]) == virt, w, 0.0).astype(BF16)
        total += dot_nt(w, one_hot(r0 == ranki + (96 * k + 32 * y)))
    od, r = parts_of(iota((384, 1), 0), 48)
    jl, b = parts_of(r, 12)
    source = jnp.where(r < 36, b * 24 + 3 * od + jl, -1)
    w = dot_nn(one_hot(iota((384, 288), 1) == source), total.astype(BF16))
    w_last[...] = jnp.zeros((8, 16, 128), F32)
    for d in range(8):
        for n in range(3):
            tile = w[d * 48 : d * 48 + 36, n * 128 : n * 128 + 128]
            wsend[d, n * 32 : n * 32 + 32] = tile[0:32].astype(BF16)
            w_last[d, n * 4 : n * 4 + 4] = tile[32:36]
    wsend[:, 96:112] = w_last[...].astype(BF16)

    pl.semaphore_wait(barrier, 33)

    def w_copy(d):
        od = lax.rem(o + d, 8)
        return pltpu.make_async_remote_copy(
            src_ref=wsend.at[od], dst_ref=wstage.at[y * 2 + xl], send_sem=w_send, recv_sem=w_recv,
            device_id=(od, z * 4 + xh * 2 + core), device_id_type=MESH,
        )

    @pl.when(xh == xl)
    def _():
        pltpu.make_async_copy(wsend.at[o], wstage.at[y * 2 + xl], w_recv).start()

    @pl.when(xh != xl)
    def _():
        w_copy(0).start()

    def w_start(d, _):
        w_copy(d).start()
        return 0

    lax.fori_loop(1, 8, w_start, 0)

    def t_copy(d, x):
        xd = lax.rem(xl + x, 2)
        return pltpu.make_async_remote_copy(
            src_ref=tsend.at[xd], dst_ref=tbuf.at[o, xl], send_sem=t_send, recv_sem=t_recv,
            device_id=(lax.rem(o + d, 8), z * 4 + xd * 2 + core), device_id_type=MESH,
        )

    load_amps.wait()
    ia, q = parts_of(iota((216, 1), 0), 6)
    i, a = parts_of(ia, 12)
    label = pick(virtf, v * 12 + a).astype(I32) ^ pick(occf, 3 * o + i).astype(I32)
    for lane in range(3):
        rows[lane] = amps[:, lane * 128 : lane * 128 + 128]
    total = jnp.zeros((216, 384), F32)
    for kk in range(4):
        t = jnp.concatenate([rows[lane, pl.ds(kk, 216, stride=4), :] for lane in range(3)], axis=1)
        t = jnp.where((label ^ pick(occf, 4 * q + kk).astype(I32)) == virt, t, 0.0).astype(BF16)
        total += dot_nt(t, one_hot(r0 == ranki + 96 * kk))
    qd, r = parts_of(iota((288, 1), 0), 48)
    source = jnp.where(r < 36, r * 6 + qd, -1)
    t = dot_nn(one_hot(iota((288, 216), 1) == source), total.astype(BF16))
    last_rows[...] = jnp.zeros((2, 48, 128), F32)
    for q in range(6):
        for lane in range(3):
            tile = t[q * 48 : q * 48 + 36, lane * 128 : lane * 128 + 128]
            n = (q % 3) * 3 + lane
            tsend[q // 3, n * 32 : n * 32 + 32] = tile[0:32].astype(BF16)
            last_rows[q // 3, n * 4 : n * 4 + 4] = tile[32:36]
    tsend[:, 288:336] = last_rows[...].astype(BF16)

    n = iota((288, 1), 0)
    gather_last[...] = one_hot(iota((288, 384), 1) == ((n & 31) >> 2) * 48 + (n >> 5) * 4 + (n & 3))
    x, n = parts_of(n, 144)
    u, r = parts_of(n, 36)
    block = u * 2 + x
    to_rows[...] = one_hot(iota((288, 288), 1) == jnp.where(r < 32, block * 32 + r, 224 + block * 4 + r))
    u, r = parts_of(iota((192, 1), 0), 48)
    i, a = r >> 4, r & 15
    to_owner[...] = one_hot(iota((192, 144), 1) == jnp.where(a < 12, u * 36 + i * 12 + a, -1))

    values = jnp.concatenate([jnp.broadcast_to(rank, (4, 384)), jnp.broadcast_to(virtf, (4, 384))], axis=0).astype(BF16)
    zz, r = parts_of(iota((1, 1280), 1), 160)
    c, r = parts_of(r, 80)
    x = jnp.where(r < 64, r >> 5, (r - 64) >> 2)
    jl, bl = parts_of(jnp.where(r < 64, r & 31, 32 + (r & 3)), 12)
    b = ((z + zz + 6) & 7) * 48 + x * 24 + c * 12 + bl
    spread = dot_nn(values, one_hot(iota((384, 1280), 0) == b)).astype(I32)
    place[...] = one_hot(iota((384, 1280), 0) == spread[0:1, :] + jl * 128)
    oj = jnp.where(jl == 0, occ_s[3 * o], jnp.where(jl == 1, occ_s[3 * o + 1], occ_s[3 * o + 2]))
    labels[...] = jnp.broadcast_to(jnp.where(r < 72, spread[4:5, :] ^ oj, -1), (8, 1280))

    x, n = parts_of(iota((288, 1), 0), 144)
    u, r = parts_of(n, 36)
    il, a = parts_of(r, 12)
    label = pick(virtf, z * 48 + x * 24 + core * 12 + a).astype(I32)
    for half in range(2):
        own = label ^ pick(occf, 12 * half + 3 * u + il).astype(I32)
        row_labels[half] = jnp.broadcast_to(own, (288, 128))

    expand[...] = one_hot((iota((256, 384), 0) & 127) == ranki)
    occ_en, virt_en = occ_e[...].reshape(1, 24), virt_e[...].reshape(1, 384)
    for i in range(3):
        a, j = parts_of(iota((288, 1), 0), 24)
        at = pl.ds(i * 288, 288)
        own = jnp.full((288, 1), 3 * o + i)
        label = pick(virtf, v * 12 + a).astype(I32) ^ pick(occf, j).astype(I32) ^ pick(occf, own).astype(I32)
        denom = pick(occ_en, own) + pick(occ_en, j) - pick(virt_en, v * 12 + a) - virt_en
        gain[at, :] = jnp.where(label == virt, 1.0 / denom, 0.0)
        amps[at, :] = jnp.where(label == virt, amps[at, :], 0.0)

    n = iota((96, 1), 0)
    zz, r = parts_of(n, 24)
    gather = one_hot(iota((96, 128), 1) == (zz * 2 + ((r & 7) >> 2)) * 16 + (r >> 3) * 4 + (r & 3))
    pltpu.make_async_copy(wstage, wstage, w_recv).wait()
    tails = dot_nn(gather, wstage[:, 96:112].reshape(128, 128))
    last = None
    zero = jnp.zeros((8, 128), F32)
    for yy in range(4):
        piece = []
        for n in range(3):
            main = wstage[yy * 2 : yy * 2 + 2, n * 32 : n * 32 + 32].reshape(64, 128).astype(F32)
            at = yy * 24 + n * 8
            piece.append(jnp.concatenate([main, tails[at : at + 8], zero], axis=0))
        first = piece[0] if last is None else piece[0] + last
        wring[2, core, :, yy * 256 : yy * 256 + 128] = first.astype(BF16)
        wring[2, core, :, yy * 256 + 128 : yy * 256 + 256] = piece[1].astype(BF16)
        last = piece[2]
    wring[2, core, :, 1024:1152] = last.astype(BF16)

    def half_block(way, t, c):
        return wring.at[(2 - way * t) % 8, c]

    def piece_of(way, t, g):
        return wring.at[(2 - way * t) % 8, core, pl.ds(pl.multiple_of(16 * g, 16), 16)]

    def ring_copy(way, t, g):
        w = (1 - way) // 2
        return pltpu.make_async_remote_copy(
            src_ref=piece_of(way, t - 1, g), dst_ref=piece_of(way, t, g),
            send_sem=ring_send.at[w * 4 + t - 1], recv_sem=ring_recv.at[w * 20 + 5 * t - 5 + g],
            device_id=(o, lax.rem(z + way + 8, 8) * 4 + s), device_id_type=MESH,
        )

    def ring_arrived(way, t, g):
        ref = piece_of(way, t, g)
        pltpu.make_async_copy(ref, ref, ring_recv.at[(1 - way) // 2 * 20 + 5 * t - 5 + g]).wait()

    def to_sibling(ref, n):
        return pltpu.make_async_remote_copy(
            src_ref=ref, dst_ref=ref, send_sem=sib_send.at[n], recv_sem=sib_recv.at[n],
            device_id=(o, z * 4 + xl * 2 + 1 - core), device_id_type=MESH,
        )

    def sib_copy(way, t, g):
        return to_sibling(piece_of(way, t, g), (1 - way) // 2 * 3 + t if t < 4 else 7)

    def sib_arrived(ref, n):
        pltpu.make_async_copy(ref, ref, sib_recv.at[n]).wait()

    def each(count, body):
        def run(g, _):
            body(g)
            return 0
        lax.fori_loop(0, count, run, 0)

    def begin(g):
        ring_copy(1, 1, g).start()
        ring_copy(-1, 1, g).start()

    each(5, begin)
    to_sibling(wring.at[2, core], 0).start()
    pltpu.make_async_copy(tsend.at[xl], tbuf.at[o, xl], t_recv).start()
    for n in range(15):
        t_copy((n + 1) // 2, (n + 1) % 2).start()
    for t in range(1, 4):
        def pass_on(g, t=t):
            for way in (1, -1):
                ring_arrived(way, t, g)
                if t < 3:
                    ring_copy(way, t + 1, g).start()
                else:
                    @pl.when(core == (1 - way) // 2)
                    def _(way=way):
                        ring_copy(way, 4, g).start()
                sib_copy(way, t, g).start()

        each(5, pass_on)

    pltpu.make_async_copy(tbuf, tbuf, t_recv).wait()

    def near(half, _):
        tiles = tbuf[pl.ds(4 * half, 4)].reshape(8, 336, 128)
        last = dot_nn(gather_last[...], tiles[:, 288:336].reshape(384, 128)).astype(BF16)
        rows36 = jnp.concatenate(
            [
                jnp.concatenate([tiles[:, n * 32 : n * 32 + 32].reshape(256, 128), last[n * 32 : n * 32 + 32]], axis=0)
                for n in range(9)
            ],
            axis=1,
        )
        left[half] = dot_nn(to_rows[...], rows36).astype(BF16)
        return 0

    lax.fori_loop(0, 2, near, 0)

    for way in (1, -1):
        @pl.when(core == (1 - way) // 2)
        def _(way=way):
            def keep(g):
                ring_arrived(way, 4, g)
                sib_copy(way, 4, g).start()

            each(5, keep)
    sib_arrived(wring.at[2, 1 - core], 0)
    for way in (1, -1):
        for t in range(1, 4):
            sib_arrived(half_block(way, t, 1 - core), (1 - way) // 2 * 3 + t)
    sib_arrived(half_block(1, 4, 1 - core), 7)

    def r_copy(c):
        half = lax.rem(xh + 1 + c, 2)
        return pltpu.make_async_remote_copy(
            src_ref=rpart.at[1 - xl, half], dst_ref=rpeer.at[half],
            send_sem=r_send.at[c], recv_sem=r_recv.at[c],
            device_id=(o, z * 4 + (1 - xl) * 2 + core), device_id_type=MESH,
        )

    def product(c, _):
        half = lax.rem(xh + 1 + c, 2)
        raw = dot_nt(left[half], wring[...].reshape(1280, 1152))
        raw = jnp.where(row_labels[half][:, 0:1] == labels[0:1, :], raw, 0.0).astype(BF16)
        both = dot_nt(raw, place[...]).astype(BF16)
        rpart[0, half] = both[0:144]
        rpart[1, half] = both[144:288]
        r_copy(c).start()
        return 0

    lax.fori_loop(0, 2, product, 0)

    def d_copy(od):
        return pltpu.make_async_remote_copy(
            src_ref=dsend.at[od], dst_ref=dbuf.at[o], send_sem=d_send, recv_sem=d_recv,
            device_id=(od, v), device_id_type=MESH,
        )

    d_local = pltpu.make_async_copy(dsend.at[o], dbuf.at[o], d_recv)

    def combine(c, _):
        half = lax.rem(xh + 1 + c, 2)
        r_copy(c).wait_recv()
        both = rpart[xl, half].astype(F32) + rpeer[half].astype(F32)
        dsend[pl.ds(4 * half, 4)] = dot_nn(to_owner[...], both.astype(BF16)).astype(BF16).reshape(4, 48, 384)
        for u in range(4):
            od = 4 * half + lax.rem(y + 1 + u, 4)

            @pl.when(od == o)
            def _():
                d_local.start()

            @pl.when(od != o)
            def _(od=od):
                d_copy(od).start()
        return 0

    lax.fori_loop(0, 2, combine, 0)
    pltpu.make_async_copy(dbuf, dbuf, d_recv).wait()

    def differ(g, _):
        for jl in range(3):
            direct = dbuf[g, :, jl * 128 : jl * 128 + 128].astype(F32)
            for i in range(3):
                change = direct[i * 16 : i * 16 + 16] - dsend[g, jl * 16 : jl * 16 + 16, i * 128 : i * 128 + 128].astype(F32)
                high = change.astype(BF16)
                diff[i, 3 * g + jl, :, 0:128] = high
                diff[i, 3 * g + jl, :, 128:256] = (change - high.astype(F32)).astype(BF16)
        return 0

    lax.fori_loop(0, 8, differ, 0)
    stores = []
    for i in range(3):
        at = pl.ds(i * 288, 288)
        e = dot_nn(diff[i].reshape(384, 256), expand[...])
        for j in range(24):
            for lane in range(3):
                rows[lane, pl.ds(i * 288 + j, 12, stride=24), :] = e[j * 16 : j * 16 + 12, lane * 128 : lane * 128 + 128]
        for lane in range(3):
            to = slice(lane * 128, lane * 128 + 128)
            amps[at, to] = amps[at, to] + rows[lane, at, :] * gain[at, to]
        stores.append(pltpu.make_async_copy(amps.at[at], out.at[at], in_sems.at[i]))
        stores[i].start()

    @pl.when(xh != xl)
    def _():
        w_copy(0).wait_send()

    def sent(d, _):
        w_copy(d).wait_send()
        t_copy(d, 0).wait_send()
        t_copy(d, 1).wait_send()
        d_copy(lax.rem(o + d, 8)).wait_send()
        return 0

    lax.fori_loop(1, 8, sent, 0)
    t_copy(0, 1).wait_send()
    to_sibling(wring.at[2, core], 0).wait_send()
    for way in (1, -1):
        for t in range(1, 4):
            def left_here(g, way=way, t=t):
                ring_copy(way, t, g).wait_send()
                sib_copy(way, t, g).wait_send()

            each(5, left_here)

        @pl.when(core == (1 - way) // 2)
        def _(way=way):
            def far_left(g):
                ring_copy(way, 4, g).wait_send()
                sib_copy(way, 4, g).wait_send()

            each(5, far_left)

    for c in range(2):
        r_copy(c).wait_send()
    for store in stores:
        store.wait()


def local(amplitudes, cycle_integrals, occ_energy, virt_energy, occ_irrep, virt_irrep):
    smem = pl.BlockSpec(memory_space=pltpu.SMEM)
    amps = jnp.transpose(amplitudes, (0, 2, 1, 3)).reshape(864, 384)
    ints = jnp.transpose(cycle_integrals, (0, 2, 1, 3))
    dma = pltpu.SemaphoreType.DMA
    hbm = pl.BlockSpec(memory_space=pltpu.HBM)
    out = pl.pallas_call(
        cycle_kernel,
        out_shape=jax.ShapeDtypeStruct((864, 384), F32),
        in_specs=[hbm, hbm, smem, hbm, hbm, hbm, hbm],
        out_specs=hbm,
        scratch_shapes=[
            pltpu.VMEM((24,), I32),
            pltpu.VMEM((384,), I32),
            pltpu.VMEM((24,), F32),
            pltpu.VMEM((384,), F32),
            pltpu.VMEM((864, 384), F32),
            pltpu.VMEM((256, 384), BF16),
            pltpu.VMEM((3, 24, 16, 256), BF16),
            pltpu.VMEM((864, 384), F32),
            pltpu.VMEM((12, 3, 24, 384), BF16),
            pltpu.VMEM((3, 864, 128), F32),
            pltpu.VMEM((2, 336, 128), BF16),
            pltpu.VMEM((8, 16, 128), F32),
            pltpu.VMEM((8, 112, 128), BF16),
            pltpu.VMEM((8, 112, 128), BF16),
            pltpu.VMEM((8, 2, 336, 128), BF16),
            pltpu.VMEM((8, 2, 80, 1152), BF16),
            pltpu.VMEM((384, 1280), BF16),
            pltpu.VMEM((8, 1280), I32),
            pltpu.VMEM((2, 48, 128), F32),
            pltpu.VMEM((288, 384), BF16),
            pltpu.VMEM((288, 288), BF16),
            pltpu.VMEM((192, 144), BF16),
            pltpu.VMEM((2, 288, 128), I32),
            pltpu.VMEM((2, 288, 1152), BF16),
            pltpu.VMEM((2, 2, 144, 384), BF16),
            pltpu.VMEM((2, 144, 384), BF16),
            pltpu.VMEM((8, 48, 384), BF16),
            pltpu.VMEM((8, 48, 384), BF16),
            dma, dma, dma, dma, dma((8,)), dma((40,)), dma((8,)), dma((8,)),
            dma((2,)), dma((2,)), dma, dma, dma((6,)),
        ],
        compiler_params=pltpu.CompilerParams(
            collective_id=0, has_side_effects=True, vmem_limit_bytes=VMEM_LIMIT
        ),
    )(amps, ints, occ_irrep, occ_irrep, virt_irrep, occ_energy, virt_energy)
    return jnp.transpose(out.reshape(3, 12, 24, 384), (0, 2, 1, 3))


def solution(mesh):
    return jax.shard_map(
        local,
        mesh=mesh,
        in_specs=(P("occ", None, "virt", None), P("virt", None, "occ", None), P(), P(), P(), P()),
        out_specs=P("occ", None, "virt", None),
        check_vma=False,
    )
```

time: 57.4 us -> 56.4 us (0.983)
  Pallas kernels: 54.8 us -> 53.8 us
    pallas_call x1, Pallas kernels: 54.8 us -> 53.8 us  [local(): pl.pallas_call(cycle_kernel, out_shape=jax.ShapeDtypeStruct((864, 384), F...]
where the time goes in v4:
time: 56.4 us; the launch traced here: 56.3 us
  Pallas kernels  53.8 us (95%)
  local copies, waits for them, and re-layouts  2.47 us (4%)
    pallas_call x1, Pallas kernels, local(): pl.pallas_call(cycle_kernel, out_shape=jax.ShapeDtypeStruct((864, 384), F...  53.8 us
    unnamed x1, local copies, waits for them, and re-layouts  2.47 us

profile of v4, /device:TPU:1, one launch (start us, length us, event | category | flops | bytes accessed | tf_op | source)
XLA Modules:
  0.0 56.3 jit_solution(15574299833439122287)
XLA Ops:
  0.0 53.8 %shard_map.64 = f32[864,384]{1,0:T(8,128)} custom-call(f32[864,384]{1,0:T(8,128)} %bitcast.8, bf16[12,3,24,384]{3,2,1,0:T(8,128)(2,1)} %bitcast.9, s32[24]{0:T(128)} %occ_h.1, s32[24]{0:T(128)} %occ_h.1, s32[384]{0:T(512)} %virt_h.1, f32[24]{0:T(128)} %occ_eh.1, f32[384]{0:T(512)} %virt_eh.1), custom_call_target="tpu_custom_call" | custom-call | tf_op jit(solution)/shard_map/pallas_call | solution.py:421
  53.8 2.5 %copy.8 = f32[3,24,12,384]{3,1,2,0:T(8,128)} copy(f32[3,24,12,384]{3,1,2,0:T(8,128)} %bitcast.7) | data formatting | bytes 2654208

commit v5 on v4

--- a/solution.py
+++ b/solution.py
@@ -44,7 +44,7 @@
 def cycle_kernel(
     amps_h, ints_h, occ_s, occ_h, virt_h, occ_eh, virt_eh, out,
     occ_r, virt_r, occ_e, virt_e, gain, expand, diff, amps, ints, rows, tsend, w_last, wsend, wstage, tbuf, wring, place, labels, last_rows, gather_last, to_rows, to_owner, row_labels,
-    left, rpart, rpeer, dsend, dbuf,
+    left, w_tail, rpart, rpeer, dsend, dbuf,
     w_send, w_recv, t_send, t_recv, ring_send, ring_recv, sib_send, sib_recv,
     r_send, r_recv, d_send, d_recv, in_sems,
 ):
@@ -166,15 +166,16 @@
     to_owner[...] = one_hot(iota((192, 144), 1) == jnp.where(a < 12, u * 36 + i * 12 + a, -1))
 
     values = jnp.concatenate([jnp.broadcast_to(rank, (4, 384)), jnp.broadcast_to(virtf, (4, 384))], axis=0).astype(BF16)
-    zz, r = parts_of(iota((1, 1280), 1), 160)
-    c, r = parts_of(r, 80)
-    x = jnp.where(r < 64, r >> 5, (r - 64) >> 2)
-    jl, bl = parts_of(jnp.where(r < 64, r & 31, 32 + (r & 3)), 12)
+    n = iota((1, 1152), 1)
+    block = jnp.where(n < 1024, n >> 6, (n - 1024) >> 3)
+    zz, c = block >> 1, block & 1
+    x = jnp.where(n < 1024, (n & 63) >> 5, (n & 7) >> 2)
+    jl, bl = parts_of(jnp.where(n < 1024, n & 31, 32 + (n & 3)), 12)
     b = ((z + zz + 6) & 7) * 48 + x * 24 + c * 12 + bl
-    spread = dot_nn(values, one_hot(iota((384, 1280), 0) == b)).astype(I32)
-    place[...] = one_hot(iota((384, 1280), 0) == spread[0:1, :] + jl * 128)
+    spread = dot_nn(values, one_hot(iota((384, 1152), 0) == b)).astype(I32)
+    place[...] = one_hot(iota((384, 1152), 0) == spread[0:1, :] + jl * 128)
     oj = jnp.where(jl == 0, occ_s[3 * o], jnp.where(jl == 1, occ_s[3 * o + 1], occ_s[3 * o + 2]))
-    labels[...] = jnp.broadcast_to(jnp.where(r < 72, spread[4:5, :] ^ oj, -1), (8, 1280))
+    labels[...] = jnp.broadcast_to(spread[4:5, :] ^ oj, (8, 1152))
 
     x, n = parts_of(iota((288, 1), 0), 144)
     u, r = parts_of(n, 36)
@@ -200,37 +201,34 @@
     gather = one_hot(iota((96, 128), 1) == (zz * 2 + ((r & 7) >> 2)) * 16 + (r >> 3) * 4 + (r & 3))
     pltpu.make_async_copy(wstage, wstage, w_recv).wait()
     tails = dot_nn(gather, wstage[:, 96:112].reshape(128, 128))
-    last = None
-    zero = jnp.zeros((8, 128), F32)
+    main, tail = [0.0] * 9, [0.0] * 9
     for yy in range(4):
-        piece = []
         for n in range(3):
-            main = wstage[yy * 2 : yy * 2 + 2, n * 32 : n * 32 + 32].reshape(64, 128).astype(F32)
             at = yy * 24 + n * 8
-            piece.append(jnp.concatenate([main, tails[at : at + 8], zero], axis=0))
-        first = piece[0] if last is None else piece[0] + last
-        wring[2, core, :, yy * 256 : yy * 256 + 128] = first.astype(BF16)
-        wring[2, core, :, yy * 256 + 128 : yy * 256 + 256] = piece[1].astype(BF16)
-        last = piece[2]
-    wring[2, core, :, 1024:1152] = last.astype(BF16)
+            main[2 * yy + n] += wstage[yy * 2 : yy * 2 + 2, n * 32 : n * 32 + 32].reshape(64, 128).astype(F32)
+            tail[2 * yy + n] += tails[at : at + 8]
+    for n in range(9):
+        wring[2, core, n * 64 : n * 64 + 64] = main[n].astype(BF16)
+    wring[2, core, 576:656] = jnp.concatenate(tail + [jnp.zeros((8, 128), F32)], axis=0).astype(BF16)
 
     def half_block(way, t, c):
         return wring.at[(2 - way * t) % 8, c]
 
     def piece_of(way, t, g):
-        return wring.at[(2 - way * t) % 8, core, pl.ds(pl.multiple_of(16 * g, 16), 16)]
+        rows_here = pl.ds(448, 208) if isinstance(g, int) else pl.ds(pl.multiple_of(224 * g, 224), 224)
+        return wring.at[(2 - way * t) % 8, core, rows_here]
 
     def ring_copy(way, t, g):
         w = (1 - way) // 2
         return pltpu.make_async_remote_copy(
             src_ref=piece_of(way, t - 1, g), dst_ref=piece_of(way, t, g),
-            send_sem=ring_send.at[w * 4 + t - 1], recv_sem=ring_recv.at[w * 20 + 5 * t - 5 + g],
+            send_sem=ring_send.at[w * 4 + t - 1], recv_sem=ring_recv.at[w * 12 + 3 * t - 3 + g],
             device_id=(o, lax.rem(z + way + 8, 8) * 4 + s), device_id_type=MESH,
         )
 
     def ring_arrived(way, t, g):
         ref = piece_of(way, t, g)
-        pltpu.make_async_copy(ref, ref, ring_recv.at[(1 - way) // 2 * 20 + 5 * t - 5 + g]).wait()
+        pltpu.make_async_copy(ref, ref, ring_recv.at[(1 - way) // 2 * 12 + 3 * t - 3 + g]).wait()
 
     def to_sibling(ref, n):
         return pltpu.make_async_remote_copy(
@@ -248,13 +246,14 @@
         def run(g, _):
             body(g)
             return 0
-        lax.fori_loop(0, count, run, 0)
+        lax.fori_loop(0, count - 1, run, 0)
+        body(count - 1)
 
     def begin(g):
         ring_copy(1, 1, g).start()
         ring_copy(-1, 1, g).start()
 
-    each(5, begin)
+    each(3, begin)
     to_sibling(wring.at[2, core], 0).start()
     pltpu.make_async_copy(tsend.at[xl], tbuf.at[o, xl], t_recv).start()
     for n in range(15):
@@ -271,7 +270,7 @@
                         ring_copy(way, 4, g).start()
                 sib_copy(way, t, g).start()
 
-        each(5, pass_on)
+        each(3, pass_on)
 
     pltpu.make_async_copy(tbuf, tbuf, t_recv).wait()
 
@@ -297,7 +296,7 @@
                 ring_arrived(way, 4, g)
                 sib_copy(way, 4, g).start()
 
-            each(5, keep)
+            each(3, keep)
     sib_arrived(wring.at[2, 1 - core], 0)
     for way in (1, -1):
         for t in range(1, 4):
@@ -305,7 +304,7 @@
     sib_arrived(half_block(1, 4, 1 - core), 7)
 
     def r_copy(c):
-        half = lax.rem(xh + 1 + c, 2)
+        half = lax.rem(xh + c, 2)
         return pltpu.make_async_remote_copy(
             src_ref=rpart.at[1 - xl, half], dst_ref=rpeer.at[half],
             send_sem=r_send.at[c], recv_sem=r_recv.at[c],
@@ -313,8 +312,10 @@
         )
 
     def product(c, _):
-        half = lax.rem(xh + 1 + c, 2)
-        raw = dot_nt(left[half], wring[...].reshape(1280, 1152))
+        half = lax.rem(xh + c, 2)
+        blocks = [wring[:, :, n * 64 : n * 64 + 64].reshape(1024, 128) for n in range(9)]
+        right = jnp.concatenate([jnp.concatenate(blocks, axis=1), w_tail[...]], axis=0)
+        raw = dot_nt(left[half], right)
         raw = jnp.where(row_labels[half][:, 0:1] == labels[0:1, :], raw, 0.0).astype(BF16)
         both = dot_nt(raw, place[...]).astype(BF16)
         rpart[0, half] = both[0:144]
@@ -322,59 +323,10 @@
         r_copy(c).start()
         return 0
 
+    last_tiles = wring[:, :, 576:656].astype(F32).reshape(16, 10, 8, 128)
+    for n in range(9):
+        w_tail[:, n * 128 : n * 128 + 128] = last_tiles[:, n].reshape(128, 128).astype(BF16)
     lax.fori_loop(0, 2, product, 0)
-
-    def d_copy(od):
-        return pltpu.make_async_remote_copy(
-            src_ref=dsend.at[od], dst_ref=dbuf.at[o], send_sem=d_send, recv_sem=d_recv,
-            device_id=(od, v), device_id_type=MESH,
-        )
-
-    d_local = pltpu.make_async_copy(dsend.at[o], dbuf.at[o], d_recv)
-
-    def combine(c, _):
-        half = lax.rem(xh + 1 + c, 2)
-        r_copy(c).wait_recv()
-        both = rpart[xl, half].astype(F32) + rpeer[half].astype(F32)
-        dsend[pl.ds(4 * half, 4)] = dot_nn(to_owner[...], both.astype(BF16)).astype(BF16).reshape(4, 48, 384)
-        for u in range(4):
-            od = 4 * half + lax.rem(y + 1 + u, 4)
-
-            @pl.when(od == o)
-            def _():
-                d_local.start()
-
-            @pl.when(od != o)
-            def _(od=od):
-                d_copy(od).start()
-        return 0
-
-    lax.fori_loop(0, 2, combine, 0)
-    pltpu.make_async_copy(dbuf, dbuf, d_recv).wait()
-
-    def differ(g, _):
-        for jl in range(3):
-            direct = dbuf[g, :, jl * 128 : jl * 128 + 128].astype(F32)
-            for i in range(3):
-                change = direct[i * 16 : i * 16 + 16] - dsend[g, jl * 16 : jl * 16 + 16, i * 128 : i * 128 + 128].astype(F32)
-                high = change.astype(BF16)
-                diff[i, 3 * g + jl, :, 0:128] = high
-                diff[i, 3 * g + jl, :, 128:256] = (change - high.astype(F32)).astype(BF16)
-        return 0
-
-    lax.fori_loop(0, 8, differ, 0)
-    stores = []
-    for i in range(3):
-        at = pl.ds(i * 288, 288)
-        e = dot_nn(diff[i].reshape(384, 256), expand[...])
-        for j in range(24):
-            for lane in range(3):
-                rows[lane, pl.ds(i * 288 + j, 12, stride=24), :] = e[j * 16 : j * 16 + 12, lane * 128 : lane * 128 + 128]
-        for lane in range(3):
-            to = slice(lane * 128, lane * 128 + 128)
-            amps[at, to] = amps[at, to] + rows[lane, at, :] * gain[at, to]
-        stores.append(pltpu.make_async_copy(amps.at[at], out.at[at], in_sems.at[i]))
-        stores[i].start()
 
     @pl.when(xh != xl)
     def _():
@@ -384,7 +336,6 @@
         w_copy(d).wait_send()
         t_copy(d, 0).wait_send()
         t_copy(d, 1).wait_send()
-        d_copy(lax.rem(o + d, 8)).wait_send()
         return 0
 
     lax.fori_loop(1, 8, sent, 0)
@@ -396,7 +347,7 @@
                 ring_copy(way, t, g).wait_send()
                 sib_copy(way, t, g).wait_send()
 
-            each(5, left_here)
+            each(3, left_here)
 
         @pl.when(core == (1 - way) // 2)
         def _(way=way):
@@ -404,8 +355,71 @@
                 ring_copy(way, 4, g).wait_send()
                 sib_copy(way, 4, g).wait_send()
 
-            each(5, far_left)
-
+            each(3, far_left)
+
+    def d_copy(od, c):
+        return pltpu.make_async_remote_copy(
+            src_ref=dsend.at[od], dst_ref=dbuf.at[o], send_sem=d_send, recv_sem=d_recv.at[c],
+            device_id=(od, v), device_id_type=MESH,
+        )
+
+    d_local = pltpu.make_async_copy(dsend.at[o], dbuf.at[o], d_recv.at[0])
+
+    def combine(c, _):
+        half = lax.rem(xh + c, 2)
+        r_copy(c).wait_recv()
+        both = rpart[xl, half].astype(F32) + rpeer[half].astype(F32)
+        dsend[pl.ds(4 * half, 4)] = dot_nn(to_owner[...], both.astype(BF16)).astype(BF16).reshape(4, 48, 384)
+        for u in range(4):
+            od = 4 * half + lax.rem(y + 1 + u, 4)
+
+            @pl.when(od == o)
+            def _():
+                d_local.start()
+
+            @pl.when(od != o)
+            def _(od=od):
+                d_copy(od, c).start()
+        return 0
+
+    lax.fori_loop(0, 2, combine, 0)
+
+    def change(c, _):
+        half = lax.rem(xh + c, 2)
+        ref = dbuf.at[pl.ds(4 * half, 4)]
+        pltpu.make_async_copy(ref, ref, d_recv.at[c]).wait()
+        for u in range(4):
+            g = 4 * half + u
+            for jl in range(3):
+                direct = dbuf[g, :, jl * 128 : jl * 128 + 128].astype(F32)
+                for i in range(3):
+                    mirror = dsend[g, jl * 16 : jl * 16 + 16, i * 128 : i * 128 + 128]
+                    x = direct[i * 16 : i * 16 + 16] - mirror.astype(F32)
+                    high = x.astype(BF16)
+                    diff[i, 3 * u + jl, :, 0:128] = high
+                    diff[i, 3 * u + jl, :, 128:256] = (x - high.astype(F32)).astype(BF16)
+        for i in range(3):
+            e = dot_nn(diff[i].reshape(192, 256), expand[...])
+            for j in range(12):
+                for lane in range(3):
+                    rows[lane, pl.ds(i * 288 + 12 * half + j, 12, stride=24), :] = e[j * 16 : j * 16 + 12, lane * 128 : lane * 128 + 128]
+        return 0
+
+    lax.fori_loop(0, 2, change, 0)
+    stores = []
+    for i in range(3):
+        at = pl.ds(i * 288, 288)
+        for lane in range(3):
+            to = slice(lane * 128, lane * 128 + 128)
+            amps[at, to] = amps[at, to] + rows[lane, at, :] * gain[at, to]
+        stores.append(pltpu.make_async_copy(amps.at[at], out.at[at], in_sems.at[i]))
+        stores[i].start()
+
+    def d_left(d, _):
+        d_copy(lax.rem(o + d, 8), 0).wait_send()
+        return 0
+
+    lax.fori_loop(1, 8, d_left, 0)
     for c in range(2):
         r_copy(c).wait_send()
     for store in stores:
@@ -430,7 +444,7 @@
             pltpu.VMEM((384,), F32),
             pltpu.VMEM((864, 384), F32),
             pltpu.VMEM((256, 384), BF16),
-            pltpu.VMEM((3, 24, 16, 256), BF16),
+            pltpu.VMEM((3, 12, 16, 256), BF16),
             pltpu.VMEM((864, 384), F32),
             pltpu.VMEM((12, 3, 24, 384), BF16),
             pltpu.VMEM((3, 864, 128), F32),
@@ -439,21 +453,22 @@
             pltpu.VMEM((8, 112, 128), BF16),
             pltpu.VMEM((8, 112, 128), BF16),
             pltpu.VMEM((8, 2, 336, 128), BF16),
-            pltpu.VMEM((8, 2, 80, 1152), BF16),
-            pltpu.VMEM((384, 1280), BF16),
-            pltpu.VMEM((8, 1280), I32),
+            pltpu.VMEM((8, 2, 656, 128), BF16),
+            pltpu.VMEM((384, 1152), BF16),
+            pltpu.VMEM((8, 1152), I32),
             pltpu.VMEM((2, 48, 128), F32),
             pltpu.VMEM((288, 384), BF16),
             pltpu.VMEM((288, 288), BF16),
             pltpu.VMEM((192, 144), BF16),
             pltpu.VMEM((2, 288, 128), I32),
             pltpu.VMEM((2, 288, 1152), BF16),
+            pltpu.VMEM((128, 1152), BF16),
             pltpu.VMEM((2, 2, 144, 384), BF16),
             pltpu.VMEM((2, 144, 384), BF16),
             pltpu.VMEM((8, 48, 384), BF16),
             pltpu.VMEM((8, 48, 384), BF16),
-            dma, dma, dma, dma, dma((8,)), dma((40,)), dma((8,)), dma((8,)),
-            dma((2,)), dma((2,)), dma, dma, dma((6,)),
+            dma, dma, dma, dma, dma((8,)), dma((24,)), dma((8,)), dma((8,)),
+            dma((2,)), dma((2,)), dma, dma((2,)), dma((6,)),
         ],
         compiler_params=pltpu.CompilerParams(
             collective_id=0, has_side_effects=True, vmem_limit_bytes=VMEM_LIMIT

time: 56.4 us -> 55.6 us (0.986)
  Pallas kernels: 53.8 us -> 53 us
    pallas_call x1, Pallas kernels: 53.8 us -> 53 us  [local(): pl.pallas_call(cycle_kernel, out_shape=jax.ShapeDtypeStruct((864, 384), F...]
where the time goes in v5:
time: 55.6 us; the launch traced here: 55.5 us
  Pallas kernels  53 us (95%)
  local copies, waits for them, and re-layouts  2.47 us (4%)
    pallas_call x1, Pallas kernels, local(): pl.pallas_call(cycle_kernel, out_shape=jax.ShapeDtypeStruct((864, 384), F...  53 us
    unnamed x1, local copies, waits for them, and re-layouts  2.47 us

profile of v5, /device:TPU:1, one launch (start us, length us, event | category | flops | bytes accessed | tf_op | source)
XLA Modules:
  0.0 55.5 jit_solution(5624817757665916515)
XLA Ops:
  0.0 53.0 %shard_map.64 = f32[864,384]{1,0:T(8,128)} custom-call(f32[864,384]{1,0:T(8,128)} %bitcast.8, bf16[12,3,24,384]{3,2,1,0:T(8,128)(2,1)} %bitcast.9, s32[24]{0:T(128)} %occ_h.1, s32[24]{0:T(128)} %occ_h.1, s32[384]{0:T(512)} %virt_h.1, f32[24]{0:T(128)} %occ_eh.1, f32[384]{0:T(512)} %virt_eh.1), custom_call_target="tpu_custom_call" | custom-call | tf_op jit(solution)/shard_map/pallas_call | solution.py:435
  53.0 2.5 %copy.8 = f32[3,24,12,384]{3,1,2,0:T(8,128)} copy(f32[3,24,12,384]{3,1,2,0:T(8,128)} %bitcast.7) | data formatting | bytes 2654208
